TPU v7x, 32 devices: a whole 2x2x4 slice. The times are simulated.
32 devices in a mesh: sec: 8 (over z, x), op: 4 (over y, core).
Axes of the slice: x: 2, y: 2, z: 4, core: 2. Of those that a mesh axis runs over, the one named last changes fastest.
Arguments:
- wavefunction: bfloat16 [16, 512, 512], P('sec'), may hold values from -24 to 24
- left_blocks: bfloat16 [16, 16, 512, 512], P('op', 'sec'), may hold values from -5 to 5
- right_blocks: bfloat16 [16, 512, 512], P('op'), may hold values from -1 to 1
- charge_shifts: int32 [16], P('op'), may hold values from -2 to 2, as said below
- sector_rows: int32 [16], replicated, may hold values from 64 to 512, as said below
Outputs:
- next_vector: bfloat16 [16, 512, 512], P('sec')
- lanczos_coefficients: float32 [2, 3], replicated
Inputs may be any that keep to these rules, and one draw needn't show every extreme that they name: `charge_shifts`: some term has offset 2, some has offset -2, and some has offset 0. `sector_rows`: multiples of 64; some sector has 512 rows.
All inputs are finite; a program needn't handle non-finite values.
Results may differ from a plain program's by a relative error of at most 0.025.
Values may be sent and summed in bfloat16 or wider, within the bound.
No kernel may reach another device: no remote copies, remote signals or barrier semaphores. Data moves between devices by JAX's collectives and lax.ppermute only.
A program may use at most 64 MiB of HBM per device.

v0:
```python
import jax
import jax.numpy as jnp
from jax import lax
from jax.sharding import PartitionSpec as P

PRODUCTS = 3


def extended(shard, sides, width):
    for axis, dim in sides:
        size, length = (lax.axis_size(axis), shard.shape[dim])
        up = [(i, (i + 1) % size) for i in range(size - 1)]
        down = [(j, i) for i, j in up]
        last = lax.slice_in_dim(shard, length - width, length, axis=dim)
        initial = lax.slice_in_dim(shard, 0, width, axis=dim)
        before = lax.ppermute(last, axis, up)
        after = lax.ppermute(initial, axis, down)
        shard = jnp.concatenate([before, shard, after], axis=dim)
    return shard


def on_device(wavefunction, left_blocks, right_blocks, charge_shifts, sector_rows):
    sectors_here, block_rows, right_width = wavefunction.shape
    terms_here = left_blocks.shape[0]
    first_sector = lax.axis_index("sec") * sectors_here
    local_rows = lax.dynamic_slice_in_dim(sector_rows, first_sector, sectors_here, 0)
    positions = jnp.arange(block_rows, dtype=jnp.int32)
    row_mask = (positions[None, :] < local_rows[:, None]).astype(jnp.float32)[:, :, None]
    live_count = right_width * jnp.sum(sector_rows).astype(jnp.float32)
    masked_start = wavefunction.astype(jnp.float32) * row_mask
    start_total = lax.psum(jnp.sum(masked_start * masked_start), "sec")
    vector = (masked_start / jnp.sqrt(start_total / live_count)).astype(jnp.bfloat16)
    alphas = []
    betas = []
    previous = jnp.zeros((sectors_here, block_rows, right_width), jnp.float32)
    beta = jnp.float32(0.0)
    for product in range(PRODUCTS):
        padded = extended(vector, (("sec", 0),), sectors_here)
        partial_value = jnp.zeros((sectors_here, block_rows, right_width), jnp.float32)
        for term in range(terms_here):
            window = lax.dynamic_slice_in_dim(
                padded, sectors_here - charge_shifts[term], sectors_here, 0
            )
            right_part = jnp.einsum(
                "sbn,nm->sbm", window, right_blocks[term], preferred_element_type=jnp.float32
            ).astype(jnp.bfloat16)
            partial_value = partial_value + jnp.einsum(
                "sab,sbm->sam", left_blocks[term], right_part, preferred_element_type=jnp.float32
            )
        image = lax.psum(partial_value.astype(jnp.bfloat16), "op").astype(jnp.float32) * row_mask
        current = vector.astype(jnp.float32)
        alpha = lax.psum(jnp.sum(current * image), "sec") / live_count
        residual = image - alpha * current - beta * previous
        beta = jnp.sqrt(lax.psum(jnp.sum(residual * residual), "sec") / live_count)
        previous = current
        vector = (residual / beta).astype(jnp.bfloat16)
        alphas.append(alpha)
        betas.append(beta)
    return (vector, jnp.stack([jnp.stack(alphas), jnp.stack(betas)]))


def solution(mesh):
    in_specs = (P("sec", None, None), P("op", "sec", None, None), P("op", None, None), P("op"), P())
    out_specs = (P("sec", None, None), P())
    return jax.shard_map(
        on_device, mesh=mesh, in_specs=in_specs, out_specs=out_specs, check_vma=False
    )
```

profile of v0, /device:TPU:0, one launch (start us, length us, event | category | flops | bytes accessed | tf_op | source)
XLA Modules:
  0.0 478.8 jit_solution(16334126614058921749)
XLA Ops:
  12.6 23.7 %psum.70 = f32[]{:T(128)} all-reduce(f32[]{:T(128)} %multiply_reduce_fusion.3), channel_id=1, replica_groups=mesh['sec'=8,'op'=4] {'sec'}, use_global_device_ids=true, to_apply=%region_1.0 | all-reduce | flops 1 | bytes 8 | tf_op jit(solution)/shard_map/psum | solution.py:31
  38.6 5.5 %collective-permute-start = (bf16[2,512,512]{1,2,0:T(8,128)(2,1)S(1)}, bf16[2,512,512]{1,2,0:T(8,128)(2,1)}, u32[]{:S(2)}, u32[]{:S(2)}) collective-permute-start(bf16[2,512,512]{1,2,0:T(8,128)(2,1)S(1)} %divide_convert_fusion.3), channel_id=1, source_target_pairs={{0,4},{4,8},{8,12},{12,16},{16,20},{20,24},{24,28},{1,5},{5,9},{9,... | collective-permute-start | bytes 3145736 | tf_op jit(solution)/shard_map/ppermute | solution.py:16
  49.9 10.5 %collective-permute-done.1 = bf16[2,512,512]{1,2,0:T(8,128)(2,1)S(1)} collective-permute-done((bf16[2,512,512]{1,2,0:T(8,128)(2,1)S(1)}, bf16[2,512,512]{1,2,0:T(8,128)(2,1)S(1)}, u32[]{:S(2)}, u32[]{:S(2)}) %collective-permute-start.1) | collective-permute-done | bytes 1048608 | tf_op jit(solution)/shard_map/ppermute | solution.py:17
  60.3 18.9 %collective-permute-done = bf16[2,512,512]{1,2,0:T(8,128)(2,1)} collective-permute-done((bf16[2,512,512]{1,2,0:T(8,128)(2,1)S(1)}, bf16[2,512,512]{1,2,0:T(8,128)(2,1)}, u32[]{:S(2)}, u32[]{:S(2)}) %collective-permute-start) | collective-permute-done | bytes 1048608 | tf_op jit(solution)/shard_map/ppermute | solution.py:16
  93.9 5.3 %fusion.8 = bf16[2,512,512]{1,2,0:T(8,128)(2,1)} fusion(f32[2,512,512]{2,1,0:T(8,128)S(1)} %fusion.13, f32[2,512,512]{2,1,0:T(8,128)} %fusion.11, f32[2,512,512]{2,1,0:T(8,128)} %fusion.12, bf16[6,512,512]{1,2,0:T(8,128)(2,1)} %pad_maximum_fusion, s32[]{:T(128)S(6)} %select_n.27, bf16[4,2,512,512]{3,2,1,0:T(8,128)(2,1)} %param.6, bf16[4,512,512]{2,1,0:T(8,128)(2,1)} %param.7), kind=kOutput, calls=%fused_computation.46 | convolution fusion | flops 1076363264 | bytes 9961476 | tf_op jit(solution)/shard_map/sab,sbm->sam/dot_general | solution.py:47
  99.3 35.5 %all-reduce.4.cloned.1.call-done = bf16[2,512,512]{1,2,0:T(8,128)(2,1)} async-done(((bf16[2,512,512]{1,2,0:T(8,128)(2,1)}), bf16[2,512,512]{1,2,0:T(8,128)(2,1)}) %all-reduce.4.cloned.1.call-update) | async-done | bytes 1048592 | tf_op jit(solution)/shard_map/psum | solution.py:50
  137.3 22.0 %psum.72 = f32[]{:T(128)} all-reduce(f32[]{:T(128)} %fusion.3), channel_id=1, replica_groups=mesh['sec'=8,'op'=4] {'sec'}, use_global_device_ids=true, to_apply=%region_5.0 | all-reduce | flops 1 | bytes 8 | tf_op jit(solution)/shard_map/psum | solution.py:52
  161.1 17.8 %psum.73 = f32[]{:T(128)} all-reduce(f32[]{:T(128)} %multiply_reduce_fusion.2), channel_id=1, replica_groups=mesh['sec'=8,'op'=4] {'sec'}, use_global_device_ids=true, to_apply=%region_7.0 | all-reduce | flops 1 | bytes 8 | tf_op jit(solution)/shard_map/psum | solution.py:54
  181.5 5.1 %collective-permute-start.2 = (bf16[2,512,512]{1,2,0:T(8,128)(2,1)S(1)}, bf16[2,512,512]{1,2,0:T(8,128)(2,1)S(1)}, u32[]{:S(2)}, u32[]{:S(2)}) collective-permute-start(bf16[2,512,512]{1,2,0:T(8,128)(2,1)S(1)} %divide_convert_fusion.2), channel_id=1, source_target_pairs={{0,4},{4,8},{8,12},{12,16},{16,20},{20,24},{24,28},{1,5},{5,9},{9,... | collective-permute-start | bytes 3145736 | tf_op jit(solution)/shard_map/ppermute | solution.py:16
  186.6 13.0 %collective-permute-done.3 = bf16[2,512,512]{1,2,0:T(8,128)(2,1)S(1)} collective-permute-done((bf16[2,512,512]{1,2,0:T(8,128)(2,1)S(1)}, bf16[2,512,512]{1,2,0:T(8,128)(2,1)S(1)}, u32[]{:S(2)}, u32[]{:S(2)}) %collective-permute-start.3) | collective-permute-done | bytes 1048608 | tf_op jit(solution)/shard_map/ppermute | solution.py:17
  199.7 22.7 %collective-permute-done.2 = bf16[2,512,512]{1,2,0:T(8,128)(2,1)S(1)} collective-permute-done((bf16[2,512,512]{1,2,0:T(8,128)(2,1)S(1)}, bf16[2,512,512]{1,2,0:T(8,128)(2,1)S(1)}, u32[]{:S(2)}, u32[]{:S(2)}) %collective-permute-start.2) | collective-permute-done | bytes 1048608 | tf_op jit(solution)/shard_map/ppermute | solution.py:16
  228.5 4.4 fusion.15
  237.2 5.9 %fusion.9 = bf16[2,512,512]{1,2,0:T(8,128)(2,1)} fusion(f32[2,512,512]{2,1,0:T(8,128)} %fusion.16, f32[2,512,512]{2,1,0:T(8,128)} %fusion.14, f32[2,512,512]{2,1,0:T(8,128)} %fusion.15, bf16[6,512,512]{1,2,0:T(8,128)(2,1)} %pad_maximum_fusion.1, s32[]{:T(128)S(6)} %select_n.27, bf16[4,2,512,512]{3,2,1,0:T(8,128)(2,1)} %param.6, bf16[4,512,512]{2,1,0:T(8,128)(2,1)} %param.7), kind=kOutput, calls=%fused_computation.47 | convolution fusion | flops 1076363264 | bytes 9961476 | tf_op jit(solution)/shard_map/sab,sbm->sam/dot_general | solution.py:47
  243.2 34.8 %all-reduce.6.cloned.1.call-done = bf16[2,512,512]{1,2,0:T(8,128)(2,1)} async-done(((bf16[2,512,512]{1,2,0:T(8,128)(2,1)}), bf16[2,512,512]{1,2,0:T(8,128)(2,1)}) %all-reduce.6.cloned.1.call-update) | async-done | bytes 1048592 | tf_op jit(solution)/shard_map/psum | solution.py:50
  280.5 22.0 %psum.75 = f32[]{:T(128)} all-reduce(f32[]{:T(128)} %fusion.6), channel_id=1, replica_groups=mesh['sec'=8,'op'=4] {'sec'}, use_global_device_ids=true, to_apply=%region_10.0 | all-reduce | flops 1 | bytes 8 | tf_op jit(solution)/shard_map/psum | solution.py:52
  304.5 17.7 %psum.76 = f32[]{:T(128)} all-reduce(f32[]{:T(128)} %multiply_reduce_fusion.1), channel_id=1, replica_groups=mesh['sec'=8,'op'=4] {'sec'}, use_global_device_ids=true, to_apply=%region_12.0 | all-reduce | flops 1 | bytes 8 | tf_op jit(solution)/shard_map/psum | solution.py:54
  326.3 4.6 collective-permute-start.4
  330.9 13.5 %collective-permute-done.5 = bf16[2,512,512]{1,2,0:T(8,128)(2,1)S(1)} collective-permute-done((bf16[2,512,512]{1,2,0:T(8,128)(2,1)S(1)}, bf16[2,512,512]{1,2,0:T(8,128)(2,1)S(1)}, u32[]{:S(2)}, u32[]{:S(2)}) %collective-permute-start.5) | collective-permute-done | bytes 1048608 | tf_op jit(solution)/shard_map/ppermute | solution.py:17
  344.4 22.6 %collective-permute-done.4 = bf16[2,512,512]{1,2,0:T(8,128)(2,1)S(1)} collective-permute-done((bf16[2,512,512]{1,2,0:T(8,128)(2,1)S(1)}, bf16[2,512,512]{1,2,0:T(8,128)(2,1)S(1)}, u32[]{:S(2)}, u32[]{:S(2)}) %collective-permute-start.4) | collective-permute-done | bytes 1048608 | tf_op jit(solution)/shard_map/ppermute | solution.py:16
  373.2 4.4 fusion.18
  382.0 5.9 %fusion.10 = bf16[2,512,512]{1,2,0:T(8,128)(2,1)} fusion(f32[2,512,512]{2,1,0:T(8,128)} %fusion.19, f32[2,512,512]{2,1,0:T(8,128)} %fusion.17, f32[2,512,512]{2,1,0:T(8,128)} %fusion.18, bf16[6,512,512]{1,2,0:T(8,128)(2,1)} %pad_maximum_fusion.2, s32[]{:T(128)S(6)} %select_n.27, bf16[4,2,512,512]{3,2,1,0:T(8,128)(2,1)} %param.6, bf16[4,512,512]{2,1,0:T(8,128)(2,1)} %param.7), kind=kOutput, calls=%fused_computation.48 | convolution fusion | flops 1076363264 | bytes 9961476 | tf_op jit(solution)/shard_map/sab,sbm->sam/dot_general | solution.py:47
  387.9 34.9 %all-reduce.8.cloned.1.call-done = bf16[2,512,512]{1,2,0:T(8,128)(2,1)} async-done(((bf16[2,512,512]{1,2,0:T(8,128)(2,1)}), bf16[2,512,512]{1,2,0:T(8,128)(2,1)}) %all-reduce.8.cloned.1.call-update) | async-done | bytes 1048592 | tf_op jit(solution)/shard_map/psum | solution.py:50
  425.2 22.0 %psum.78 = f32[]{:T(128)} all-reduce(f32[]{:T(128)} %fusion), channel_id=1, replica_groups=mesh['sec'=8,'op'=4] {'sec'}, use_global_device_ids=true, to_apply=%region_15.0 | all-reduce | flops 1 | bytes 8 | tf_op jit(solution)/shard_map/psum | solution.py:52
  449.1 17.7 %psum.79 = f32[]{:T(128)} all-reduce(f32[]{:T(128)} %multiply_reduce_fusion), channel_id=1, replica_groups=mesh['sec'=8,'op'=4] {'sec'}, use_global_device_ids=true, to_apply=%region_17.0 | all-reduce | flops 1 | bytes 8 | tf_op jit(solution)/shard_map/psum | solution.py:54
  (47 shorter events, 63.8 us)
Async XLA Ops:
  7.2 127.6 %all-reduce.4.cloned.1.call-start = ((), (), s32[]{:S(2)}) async-start(), calls=%async_computation | async-start | bytes 2097152 | tf_op jit(solution)/shard_map/psum | solution.py:50
  10.8 33.3 %copy-start.3 = (s32[4]{0:T(128)S(1)}, s32[4]{0:T(128)}, u32[]{:S(2)}) copy-start(s32[4]{0:T(128)} %param.8) | copy-start | bytes 52
  37.3 23.0 %collective-permute-start.1 = (bf16[2,512,512]{1,2,0:T(8,128)(2,1)S(1)}, bf16[2,512,512]{1,2,0:T(8,128)(2,1)S(1)}, u32[]{:S(2)}, u32[]{:S(2)}) collective-permute-start(bf16[2,512,512]{1,2,0:T(8,128)(2,1)S(1)} %divide_convert_fusion.3), channel_id=1, source_target_pairs={{4,0},{8,4},{12,8},{16,12},{20,16},{24,20},{28,24},{5,1},{9,5},{13... | collective-permute-start | bytes 3145736 | tf_op jit(solution)/shard_map/ppermute | solution.py:17
  38.6 40.7 %collective-permute-start = (bf16[2,512,512]{1,2,0:T(8,128)(2,1)S(1)}, bf16[2,512,512]{1,2,0:T(8,128)(2,1)}, u32[]{:S(2)}, u32[]{:S(2)}) collective-permute-start(bf16[2,512,512]{1,2,0:T(8,128)(2,1)S(1)} %divide_convert_fusion.3), channel_id=1, source_target_pairs={{0,4},{4,8},{8,12},{12,16},{16,20},{20,24},{24,28},{1,5},{5,9},{9,... | collective-permute-start | bytes 3145736 | tf_op jit(solution)/shard_map/ppermute | solution.py:16
  99.2 178.8 %all-reduce.6.cloned.1.call-start = ((), (), s32[]{:S(2)}) async-start(), calls=%async_computation.1 | async-start | bytes 2097152 | tf_op jit(solution)/shard_map/psum | solution.py:50
  134.8 25.1 %copy-start.2 = (bf16[2,512,512]{1,2,0:T(8,128)(2,1)S(1)}, bf16[2,512,512]{1,2,0:T(8,128)(2,1)}, u32[]{:S(2)}) copy-start(bf16[2,512,512]{1,2,0:T(8,128)(2,1)} %all-reduce.4.cloned.1.call-done) | copy-start | bytes 3145732
  180.2 19.4 %collective-permute-start.3 = (bf16[2,512,512]{1,2,0:T(8,128)(2,1)S(1)}, bf16[2,512,512]{1,2,0:T(8,128)(2,1)S(1)}, u32[]{:S(2)}, u32[]{:S(2)}) collective-permute-start(bf16[2,512,512]{1,2,0:T(8,128)(2,1)S(1)} %divide_convert_fusion.2), channel_id=1, source_target_pairs={{4,0},{8,4},{12,8},{16,12},{20,16},{24,20},{28,24},{5,1},{9,5},{13... | collective-permute-start | bytes 3145736 | tf_op jit(solution)/shard_map/ppermute | solution.py:17
  181.5 40.8 %collective-permute-start.2 = (bf16[2,512,512]{1,2,0:T(8,128)(2,1)S(1)}, bf16[2,512,512]{1,2,0:T(8,128)(2,1)S(1)}, u32[]{:S(2)}, u32[]{:S(2)}) collective-permute-start(bf16[2,512,512]{1,2,0:T(8,128)(2,1)S(1)} %divide_convert_fusion.2), channel_id=1, source_target_pairs={{0,4},{4,8},{8,12},{12,16},{16,20},{20,24},{24,28},{1,5},{5,9},{9,... | collective-permute-start | bytes 3145736 | tf_op jit(solution)/shard_map/ppermute | solution.py:16
  243.2 179.6 %all-reduce.8.cloned.1.call-start = ((), (), s32[]{:S(2)}) async-start(), calls=%async_computation.2 | async-start | bytes 2097152 | tf_op jit(solution)/shard_map/psum | solution.py:50
  278.0 25.1 %copy-start = (bf16[2,512,512]{1,2,0:T(8,128)(2,1)S(1)}, bf16[2,512,512]{1,2,0:T(8,128)(2,1)}, u32[]{:S(2)}) copy-start(bf16[2,512,512]{1,2,0:T(8,128)(2,1)} %all-reduce.6.cloned.1.call-done) | copy-start | bytes 3145732
  325.0 19.5 %collective-permute-start.5 = (bf16[2,512,512]{1,2,0:T(8,128)(2,1)S(1)}, bf16[2,512,512]{1,2,0:T(8,128)(2,1)S(1)}, u32[]{:S(2)}, u32[]{:S(2)}) collective-permute-start(bf16[2,512,512]{1,2,0:T(8,128)(2,1)S(1)} %divide_convert_fusion.1), channel_id=1, source_target_pairs={{4,0},{8,4},{12,8},{16,12},{20,16},{24,20},{28,24},{5,1},{9,5},{13... | collective-permute-start | bytes 3145736 | tf_op jit(solution)/shard_map/ppermute | solution.py:17
  326.3 40.8 %collective-permute-start.4 = (bf16[2,512,512]{1,2,0:T(8,128)(2,1)S(1)}, bf16[2,512,512]{1,2,0:T(8,128)(2,1)S(1)}, u32[]{:S(2)}, u32[]{:S(2)}) collective-permute-start(bf16[2,512,512]{1,2,0:T(8,128)(2,1)S(1)} %divide_convert_fusion.1), channel_id=1, source_target_pairs={{0,4},{4,8},{8,12},{12,16},{16,20},{20,24},{24,28},{1,5},{5,9},{9,... | collective-permute-start | bytes 3145736 | tf_op jit(solution)/shard_map/ppermute | solution.py:16
  422.8 25.1 %copy-start.1 = (bf16[2,512,512]{1,2,0:T(8,128)(2,1)S(1)}, bf16[2,512,512]{1,2,0:T(8,128)(2,1)}, u32[]{:S(2)}) copy-start(bf16[2,512,512]{1,2,0:T(8,128)(2,1)} %all-reduce.8.cloned.1.call-done) | copy-start | bytes 3145732
Sparse Core Ops, SparseCore 0:
  99.3 35.4 all-reduce.3
  243.3 34.6 all-reduce.5
  388.0 34.6 all-reduce.7
where the time goes:
time: 480 us; the launch traced here: 479 us
  waiting for transfers between devices  206 us (43%)
  blocking collectives  143 us (30%)
  matrix products  55.1 us (11%)
  other arithmetic  25.5 us (5%)
  between operations  24.4 us (5%)
  starting transfers between devices  19.2 us (4%)
  local copies, waits for them, and re-layouts  5.13 us (1%)
    psum x3, waiting for transfers between devices, on_device(): lax.psum(partial_value.astype(jnp.bfloat16), 'op').astype(jnp.float32)  105 us
    psum x3, blocking collectives, on_device(): alpha = lax.psum(jnp.sum(current * image), 'sec') / live_count  65.9 us
    ppermute x3, waiting for transfers between devices, extended(): before = lax.ppermute(last, axis, up)  64.2 us
    dot_general x12, matrix products, on_device(): jnp.einsum('sab,sbm->sam', left_blocks[term], right_part, preferred_eleme...  55.1 us
    psum x3, blocking collectives, on_device(): beta = jnp.sqrt(lax.psum(jnp.sum(residual * residual), 'sec') / live_count)  53.3 us
    ppermute x3, waiting for transfers between devices, extended(): after = lax.ppermute(initial, axis, down)  37 us
    psum x1, blocking collectives, on_device(): start_total = lax.psum(jnp.sum(masked_start * masked_start), 'sec')  23.7 us
    ppermute x3, starting transfers between devices, extended(): before = lax.ppermute(last, axis, up)  15.2 us
  transfers between devices with their start and end apart: 9, of which 9 were waited for; matrix products, arithmetic and copies ran while one was open for 0% of the time, Pallas kernels for 0%

commit v1 on v0

v1 whole, which is shorter than its diff:
```python
import functools

import jax
import jax.numpy as jnp
from jax import lax
from jax.experimental import pallas as pl
from jax.experimental.pallas import tpu as pltpu
from jax.sharding import PartitionSpec as P

PRODUCTS = 3
F32 = jnp.float32
BF16 = jnp.bfloat16
VMEM = pl.BlockSpec(memory_space=pltpu.VMEM)
SMEM = pl.BlockSpec(memory_space=pltpu.SMEM)
CORE, SEC, LIVE, ROWS, SHIFTS = 0, 1, 2, 3, 5


def call(kernel, name, out, scratch, *operands, flops=0):
    moved = sum(a.size * a.dtype.itemsize for a in operands)
    return pl.pallas_call(
        kernel,
        name=name,
        out_shape=out,
        in_specs=[SMEM] + [VMEM] * (len(operands) - 1),
        out_specs=jax.tree.map(lambda _: VMEM, out),
        scratch_shapes=scratch,
        compiler_params=pltpu.CompilerParams(vmem_limit_bytes=24 << 20),
        cost_estimate=pl.CostEstimate(flops=flops, bytes_accessed=moved, transcendentals=0),
    )(*operands)


def lane_sums(value):
    rows, columns = value.shape
    folded = sum(value[:, i : i + 128] for i in range(0, columns, 128))
    return jnp.sum(folded, axis=0, keepdims=True)


def total(stats_ref, row, live):
    return jnp.sum(stats_ref[row : row + 1, :], axis=1, keepdims=True) / live


def write_sums(stats_ref, values):
    rows = stats_ref.shape[0]
    parts = [lane_sums(v) for v in values]
    parts += [jnp.zeros((1, 128), F32)] * (rows - len(parts))
    stats_ref[...] = jnp.concatenate(parts, axis=0)


def coefficients(stats, live):
    norm = jnp.sqrt(total(stats[0], 0, live))
    alphas, betas = [], []
    for k, ref in enumerate(stats[1:]):
        alpha = total(ref, 1, live)
        square = total(ref, 0, live) - alpha * alpha
        if k:
            square = square - 2.0 * betas[-1] * total(ref, 2, live) + betas[-1] * betas[-1]
        alphas.append(alpha)
        betas.append(jnp.sqrt(jnp.maximum(square, 0.0)))
    return norm, alphas, betas


def lanczos_vectors(start, images, norm, alphas, betas):
    vectors = [start / norm]
    for k, beta in enumerate(betas):
        residual = images[k] - alphas[k] * vectors[k]
        if k:
            residual = residual - betas[k - 1] * vectors[k - 1]
        vectors.append(residual / beta)
    return vectors


def start_kernel(info, x_ref, *refs):
    *halves, stats_ref = refs
    sectors, block_rows, _ = x_ref.shape
    half = block_rows // 2
    core = info[CORE]
    square = 0.0
    for t in range(sectors):
        for which in range(2):
            first = pl.multiple_of((core if which == 0 else 1 - core) * half, half)
            value = x_ref[t, pl.ds(first, half), :]
            rows = lax.broadcasted_iota(jnp.int32, value.shape, 0) + first
            value = jnp.where(rows < info[ROWS + t], value, jnp.zeros_like(value))
            halves[2 * t + which][...] = value
            if which == 0:
                wide = value.astype(F32)
                square = square + wide * wide
    write_sums(stats_ref, [square])


def select_source(info, block, refs, v_ref):
    half = refs[0].shape[0]
    core = info[CORE]
    even = info[SEC] % 2 == 0
    mine = pl.ds(pl.multiple_of(core * half, half), half)
    other = pl.ds(pl.multiple_of((1 - core) * half, half), half)
    from_pair = (block == 1) == even
    for k, here in enumerate(
        (block == 0, (block != 0) & from_pair, (block != 0) & jnp.logical_not(from_pair))
    ):

        @pl.when(here)
        def _():
            v_ref[mine, :] = refs[2 * k][...]
            v_ref[other, :] = refs[2 * k + 1][...]


def apply_term(info, w, target, refs, left_ref, right_ref, v_ref, acc_ref):
    select_source(info, (target - info[SHIFTS + w]) >> 1, refs, v_ref)
    part = jnp.dot(v_ref[...], right_ref[w], preferred_element_type=F32).astype(BF16)
    acc_ref[...] += jnp.dot(left_ref[w, target], part, preferred_element_type=F32)


def first_kernel(info, *refs):
    *sources, left_ref, right_ref, acc_ref, v_ref = refs
    acc_ref[...] = jnp.zeros_like(acc_ref)

    def step(w, carry):
        target = info[SHIFTS + w] & 1
        apply_term(info, w, target, sources, left_ref, right_ref, v_ref, acc_ref.at[target])
        return carry

    lax.fori_loop(0, left_ref.shape[0], step, 0)


def second_kernel(target, info, *refs):
    *sources, left_ref, right_ref, sum_ref, mine_ref, other_ref, v_ref, acc_ref = refs
    half = mine_ref.shape[0]
    acc_ref[...] = sum_ref[target]

    def step(w, carry):
        @pl.when(((info[SHIFTS + w] + 1) & 1) == target)
        def _():
            apply_term(info, w, target, sources, left_ref, right_ref, v_ref, acc_ref)

        return carry

    lax.fori_loop(0, left_ref.shape[0], step, 0)
    core = info[CORE]
    mine_ref[...] = acc_ref[pl.ds(pl.multiple_of(core * half, half), half), :].astype(BF16)
    other_ref[...] = acc_ref[pl.ds(pl.multiple_of((1 - core) * half, half), half), :].astype(BF16)


def add_kernel(info, a_ref, b_ref, out_ref):
    out_ref[...] = (a_ref[...].astype(F32) + b_ref[...].astype(F32)).astype(BF16)


def image_kernel(product, target, info, *refs):
    a_ref, b_ref, start_ref = refs[:3]
    images = [r[...].astype(F32) for r in refs[3 : 3 + product]]
    stats = refs[3 + product : 4 + 2 * product]
    out_ref, stats_ref = refs[4 + 2 * product :]
    columns = out_ref.shape[1]
    live = info[LIVE].astype(F32) * columns
    norm, alphas, betas = coefficients(stats, live)
    vectors = lanczos_vectors(start_ref[...].astype(F32), images, norm, alphas, betas)
    value = a_ref[...].astype(F32) + b_ref[...].astype(F32)
    if product == 0:
        value = value / norm
    else:
        value = value - alphas[-1] * images[-1]
        if product > 1:
            value = value - betas[-2] * images[-2]
        value = value / betas[-1]
    rows = lax.broadcasted_iota(jnp.int32, value.shape, 0) + info[CORE] * value.shape[0]
    value = jnp.where(rows < info[ROWS + target], value, 0.0)
    out_ref[...] = value.astype(BF16)
    value = value.astype(BF16).astype(F32)
    sums = [value * value, value * vectors[-1]]
    if product:
        sums.append(value * vectors[-2])
    write_sums(stats_ref, sums)


def last_kernel(products, info, *refs):
    per_sector = 2 * (products + 1)
    stats = refs[-3 - products : -2]
    out_ref, coef_ref = refs[-2:]
    sectors, block_rows, columns = out_ref.shape
    half = block_rows // 2
    live = info[LIVE].astype(F32) * columns
    norm, alphas, betas = coefficients(stats, live)
    for t in range(sectors):
        for which in range(2):
            basis = [
                refs[t * per_sector + 2 * k + which][...].astype(F32) for k in range(products + 1)
            ]
            vector = lanczos_vectors(basis[0], basis[1:], norm, alphas, betas)[-1]
            core = info[CORE] if which == 0 else 1 - info[CORE]
            out_ref[t, pl.ds(pl.multiple_of(core * half, half), half), :] = vector.astype(BF16)
    row = lax.broadcasted_iota(jnp.int32, coef_ref.shape, 0)
    column = lax.broadcasted_iota(jnp.int32, coef_ref.shape, 1)
    value = jnp.zeros(coef_ref.shape, F32)
    for k in range(products):
        value = jnp.where((row == 0) & (column == k), alphas[k], value)
        value = jnp.where((row == 1) & (column == k), betas[k], value)
    coef_ref[...] = value


def on_device(wavefunction, left_blocks, right_blocks, charge_shifts, sector_rows):
    sectors, block_rows, columns = wavefunction.shape
    half = block_rows // 2
    n_sec, n_op = lax.axis_size("sec"), lax.axis_size("op")
    assert sectors == 2 and n_sec % 2 == 0 and n_op % 2 == 0
    sec, op = lax.axis_index("sec"), lax.axis_index("op")
    core_pairs = [(i, i ^ 1) for i in range(n_op)]
    pairs = [(i, i ^ 1) for i in range(n_sec)]
    onward = [(i, i + 2) for i in range(0, n_sec - 2, 2)]
    onward += [(i, i - 2) for i in range(3, n_sec, 2)]

    def across_cores(value):
        return lax.ppermute(value, "op", core_pairs)

    def sum_all(stats):
        stats = stats + across_cores(stats)
        bit = 1
        while bit < n_sec:
            stats = stats + lax.ppermute(stats, "sec", [(i, i ^ bit) for i in range(n_sec)])
            bit *= 2
        return stats

    local_rows = lax.dynamic_slice_in_dim(sector_rows, sec * sectors, sectors, 0)
    info = jnp.concatenate(
        [
            jnp.stack([op % 2, sec, jnp.sum(sector_rows)]).astype(jnp.int32),
            local_rows,
            charge_shifts,
        ]
    )
    half_type = jax.ShapeDtypeStruct((half, columns), BF16)
    stats_type = jax.ShapeDtypeStruct((8, 128), F32)
    acc_type = jax.ShapeDtypeStruct((sectors, block_rows, columns), F32)
    v_scratch = pltpu.VMEM((block_rows, columns), BF16)
    acc_scratch = pltpu.VMEM((block_rows, columns), F32)

    *halves, start_stats = call(
        start_kernel, "start", [half_type] * (2 * sectors) + [stats_type], [], info, wavefunction
    )
    basis = [[(halves[0], halves[1]), (halves[2], halves[3])]]
    stats = [sum_all(start_stats)]
    pair_flops = 4 * block_rows * block_rows * columns
    terms = left_blocks.shape[0]

    for product in range(PRODUCTS):
        sources = []
        for t in range(sectors):
            mine, other = basis[-1][t]
            pair = lax.ppermute(mine, "sec", pairs)
            far = lax.ppermute(pair, "sec", onward)
            sources.append((mine, other, pair, across_cores(pair), far, across_cores(far)))
        acc = call(
            first_kernel, "first", acc_type, [v_scratch],
            info, *sources[0], left_blocks, right_blocks, flops=terms * pair_flops,
        )
        image = []
        sums = []
        for t in range(sectors):
            mine, other = call(
                functools.partial(second_kernel, t), "second", [half_type] * 2,
                [v_scratch, acc_scratch],
                info, *sources[1], left_blocks, right_blocks, acc, flops=terms * pair_flops // 2,
            )
            value = call(add_kernel, "add", half_type, [], info, mine, across_cores(other))
            bit = 2
            while 2 * bit < n_op:
                arrived = lax.ppermute(value, "op", [(i, i ^ bit) for i in range(n_op)])
                value = call(add_kernel, "add", half_type, [], info, value, arrived)
                bit *= 2
            arrived = lax.ppermute(value, "op", [(i, i ^ bit) for i in range(n_op)])
            mine, part = call(
                functools.partial(image_kernel, product, t), "image", [half_type, stats_type], [],
                info, value, arrived, *[b[t][0] for b in basis], *stats,
            )
            image.append((mine, across_cores(mine)))
            sums.append(part)
        basis.append(image)
        stats.append(sum_all(sums[0] + sums[1]))

    flat = [h for t in range(sectors) for b in basis for h in b[t]]
    vector_type = jax.ShapeDtypeStruct(wavefunction.shape, BF16)
    coef_type = jax.ShapeDtypeStruct((2, PRODUCTS), F32)
    vector, coef = call(
        functools.partial(last_kernel, PRODUCTS), "last", [vector_type, coef_type], [],
        info, *flat, *stats,
    )
    return vector, coef


def solution(mesh):
    in_specs = (P("sec", None, None), P("op", "sec", None, None), P("op", None, None), P("op"), P())
    out_specs = (P("sec", None, None), P())
    return jax.shard_map(
        on_device, mesh=mesh, in_specs=in_specs, out_specs=out_specs, check_vma=False
    )
```

time: 480 us -> 183 us (0.38)
  waiting for transfers between devices: 206 us -> 58 us
  blocking collectives: 143 us -> 0 us
  matrix products: 55.1 us -> 0 us
  starting transfers between devices: 19.2 us -> 72.4 us
  Pallas kernels: 0 us -> 40.7 us
  other arithmetic: 25.5 us -> 1.38 us
  between operations: 24.4 us -> 1.04 us
    psum x7 -> x0, blocking collectives: 143 us -> none  [the longest x3 65.9 us: on_device(): alpha = lax.psum(jnp.sum(current * image), 'sec') / live_count]
    psum x3 -> x0, waiting for transfers between devices: 105 us -> none  [on_device(): lax.psum(partial_value.astype(jnp.bfloat16), 'op').astype(jnp.float32)]
    dot_general x12 -> x0, matrix products: 55.1 us -> none  [on_device(): jnp.einsum('sab,sbm->sam', left_blocks[term], right_part, preferred_eleme...]
    ppermute x6 -> x58, starting transfers between devices: 19.1 us -> 72.4 us  [the longest x12 28.3 us: sum_all(): lax.ppermute(stats, 'sec', [(i, i ^ bit) for i in range(n_sec)])]
    ppermute x6 -> x58, waiting for transfers between devices: 101 us -> 58 us  [the longest x12 20.2 us: sum_all(): lax.ppermute(stats, 'sec', [(i, i ^ bit) for i in range(n_sec)])]
    pallas_call x0 -> x23, Pallas kernels: none -> 40.7 us  [call(): pl.pallas_call(kernel, name=name, out_shape=out, in_specs=[SMEM] + [VMEM]...]
    reduce_sum x8 -> x1, other arithmetic: 13.7 us -> 1.32 us  [on_device(): jnp.sum(sector_rows)]
    concatenate x3 -> x0, other arithmetic: 6.49 us -> none  [extended(): shard = jnp.concatenate([before, shard, after], axis=dim)]
  transfers between devices with their start and end apart: 9 -> 58, of which waited for: 9 -> 23; matrix products, arithmetic and copies ran while one was open for 0% -> 0% of each run, Pallas kernels for 0% -> 16%
where the time goes in v1:
time: 183 us; the launch traced here: 181 us
  starting transfers between devices  72.4 us (40%)
  waiting for transfers between devices  58 us (32%)
  Pallas kernels  40.7 us (22%)
  local copies, waits for them, and re-layouts  7.07 us (4%)
    pallas_call x23, Pallas kernels, call(): pl.pallas_call(kernel, name=name, out_shape=out, in_specs=[SMEM] + [VMEM]...  40.7 us
    ppermute x12, starting transfers between devices, sum_all(): lax.ppermute(stats, 'sec', [(i, i ^ bit) for i in range(n_sec)])  28.3 us
    ppermute x6, starting transfers between devices, on_device(): far = lax.ppermute(pair, 'sec', onward)  22 us
    ppermute x12, waiting for transfers between devices, sum_all(): lax.ppermute(stats, 'sec', [(i, i ^ bit) for i in range(n_sec)])  20.2 us
    ppermute x6, waiting for transfers between devices, on_device(): pair = lax.ppermute(mine, 'sec', pairs)  19 us
    ppermute x6, waiting for transfers between devices, on_device(): far = lax.ppermute(pair, 'sec', onward)  14.3 us
    ppermute x6, starting transfers between devices, on_device(): arrived = lax.ppermute(value, 'op', [(i, i ^ bit) for i in range(n_op)])  8.95 us
    ppermute x6, starting transfers between devices, on_device(): pair = lax.ppermute(mine, 'sec', pairs)  7.39 us
  transfers between devices with their start and end apart: 58, of which 23 were waited for; matrix products, arithmetic and copies ran while one was open for 0% of the time, Pallas kernels for 16%

profile of v1, /device:TPU:0, one launch (start us, length us, event | category | flops | bytes accessed | tf_op | source)
XLA Modules:
  0.0 180.6 jit_solution(15948566381253002623)
XLA Ops:
  6.0 3.0 %collective-permute-start.4 = (bf16[256,512]{1,0:T(8,128)(2,1)S(1)}, bf16[256,512]{1,0:T(8,128)(2,1)S(1)}, u32[]{:S(2)}, u32[]{:S(2)}) collective-permute-start(bf16[256,512]{1,0:T(8,128)(2,1)S(1)} %get-tuple-element.31.refs_0_.refs_2_), channel_id=1, source_target_pairs={{0,4},{4,0},{8,12},{12,8},{16,20},{20,16},{24,28},{28,24},{1,5},{5... | collective-permute-start | bytes 786440 | tf_op jit(solution)/shard_map/ppermute | solution.py:248
  9.1 7.1 %collective-permute-done.4.refs_2_ = bf16[256,512]{1,0:T(8,128)(2,1)S(1)} collective-permute-done((bf16[256,512]{1,0:T(8,128)(2,1)S(1)}, bf16[256,512]{1,0:T(8,128)(2,1)S(1)}, u32[]{:S(2)}, u32[]{:S(2)}) %collective-permute-start.4) | collective-permute-done | bytes 262176 | tf_op jit(solution)/shard_map/ppermute | solution.py:248
  16.1 4.1 %collective-permute-start.6 = (bf16[256,512]{1,0:T(8,128)(2,1)S(1)}, bf16[256,512]{1,0:T(8,128)(2,1)S(1)}, u32[]{:S(2)}, u32[]{:S(2)}) collective-permute-start(bf16[256,512]{1,0:T(8,128)(2,1)S(1)} %collective-permute-done.4.refs_2_), channel_id=1, source_target_pairs={{0,8},{8,16},{16,24},{12,4},{20,12},{28,20},{1,9},{9,17},{17,25},{... | collective-permute-start | bytes 786440 | tf_op jit(solution)/shard_map/ppermute | solution.py:249
  20.9 3.7 %collective-permute-start.2 = (bf16[256,512]{1,0:T(8,128)(2,1)S(1)}, bf16[256,512]{1,0:T(8,128)(2,1)S(1)}, u32[]{:S(2)}, u32[]{:S(2)}) collective-permute-start(bf16[256,512]{1,0:T(8,128)(2,1)S(1)} %collective-permute-done.refs_2_), channel_id=1, source_target_pairs={{0,8},{8,16},{16,24},{12,4},{20,12},{28,20},{1,9},{9,17},{17,25},{... | collective-permute-start | bytes 786440 | tf_op jit(solution)/shard_map/ppermute | solution.py:249
  25.3 4.3 %collective-permute-done.2.refs_4_ = bf16[256,512]{1,0:T(8,128)(2,1)S(1)} collective-permute-done((bf16[256,512]{1,0:T(8,128)(2,1)S(1)}, bf16[256,512]{1,0:T(8,128)(2,1)S(1)}, u32[]{:S(2)}, u32[]{:S(2)}) %collective-permute-start.2) | collective-permute-done | bytes 262176 | tf_op jit(solution)/shard_map/ppermute | solution.py:249
  33.5 4.0 %first.3.refs_8_ = f32[2,512,512]{2,1,0:T(8,128)S(1)} custom-call(s32[9]{0:T(128)S(1)} %concatenate.3.info, bf16[256,512]{1,0:T(8,128)(2,1)S(1)} %get-tuple-element.31.refs_0_.refs_2_, bf16[256,512]{1,0:T(8,128)(2,1)S(1)} %get-tuple-element.32.refs_1_, bf16[256,512]{1,0:T(8,128)(2,1)S(1)} %collective-permute-done.4.refs_2_, ...), custom_call_target="tpu_custom_call" | custom-call | flops 2147483648 | bytes 7864356 | tf_op jit(solution)/shard_map/first/pallas_call | solution.py:20
  39.7 3.2 %second.7 = (bf16[256,512]{1,0:T(8,128)(2,1)S(1)}, bf16[256,512]{1,0:T(8,128)(2,1)S(1)}) custom-call(s32[9]{0:T(128)S(1)} %concatenate.3.info, bf16[256,512]{1,0:T(8,128)(2,1)S(1)} %get-tuple-element.33.refs_0_.refs_2_.refs_8_, bf16[256,512]{1,0:T(8,128)(2,1)S(1)} %get-tuple-element.34.refs_1_.refs_9_, bf16[256,512]{1,0:T(8,128)(2,1)S(1)} %collective-permute-done.refs_2_, ...), custom_call_target="tpu_custom_call" | custom-call | flops 1073741824 | bytes 9961508 | tf_op jit(solution)/shard_map/second/pallas_call | solution.py:20
  56.4 3.0 %collective-permute-start.13 = (f32[8,128]{1,0:T(8,128)S(1)}, f32[8,128]{1,0:T(8,128)S(1)}, u32[]{:S(2)}, u32[]{:S(2)}) collective-permute-start(f32[8,128]{1,0:T(8,128)S(1)} %add.74), channel_id=1, source_target_pairs={{0,16},{4,20},{8,24},{12,28},{16,0},{20,4},{24,8},{28,12},{1,17},{... | collective-permute-start | bytes 12296 | tf_op jit(solution)/shard_map/ppermute | solution.py:218
  64.9 5.7 %collective-permute-done.22.refs_2_ = bf16[256,512]{1,0:T(8,128)(2,1)S(1)} collective-permute-done((bf16[256,512]{1,0:T(8,128)(2,1)S(1)}, bf16[256,512]{1,0:T(8,128)(2,1)S(1)}, u32[]{:S(2)}, u32[]{:S(2)}) %collective-permute-start.22) | collective-permute-done | bytes 262176 | tf_op jit(solution)/shard_map/ppermute | solution.py:248
  70.6 3.5 %collective-permute-start.24 = (bf16[256,512]{1,0:T(8,128)(2,1)S(1)}, bf16[256,512]{1,0:T(8,128)(2,1)S(1)}, u32[]{:S(2)}, u32[]{:S(2)}) collective-permute-start(bf16[256,512]{1,0:T(8,128)(2,1)S(1)} %collective-permute-done.22.refs_2_), channel_id=1, source_target_pairs={{0,8},{8,16},{16,24},{12,4},{20,12},{28,20},{1,9},{9,17},{17,25},{... | collective-permute-start | bytes 786440 | tf_op jit(solution)/shard_map/ppermute | solution.py:249
  74.2 3.5 %collective-permute-start.20 = (bf16[256,512]{1,0:T(8,128)(2,1)S(1)}, bf16[256,512]{1,0:T(8,128)(2,1)S(1)}, u32[]{:S(2)}, u32[]{:S(2)}) collective-permute-start(bf16[256,512]{1,0:T(8,128)(2,1)S(1)} %collective-permute-done.18.refs_2_), channel_id=1, source_target_pairs={{0,8},{8,16},{16,24},{12,4},{20,12},{28,20},{1,9},{9,17},{17,25},{... | collective-permute-start | bytes 786440 | tf_op jit(solution)/shard_map/ppermute | solution.py:249
  78.8 5.1 %collective-permute-done.20.refs_4_ = bf16[256,512]{1,0:T(8,128)(2,1)S(1)} collective-permute-done((bf16[256,512]{1,0:T(8,128)(2,1)S(1)}, bf16[256,512]{1,0:T(8,128)(2,1)S(1)}, u32[]{:S(2)}, u32[]{:S(2)}) %collective-permute-start.20) | collective-permute-done | bytes 262176 | tf_op jit(solution)/shard_map/ppermute | solution.py:249
  83.9 4.0 %first.4.refs_8_ = f32[2,512,512]{2,1,0:T(8,128)S(1)} custom-call(s32[9]{0:T(128)S(1)} %concatenate.3.info, bf16[256,512]{1,0:T(8,128)(2,1)S(1)} %get-tuple-element.38.refs_0_.refs_3_.refs_2_, bf16[256,512]{1,0:T(8,128)(2,1)S(1)} %collective-permute-done.14.refs_1_.refs_3_, bf16[256,512]{1,0:T(8,128)(2,1)S(1)} %collective-permute-done.22.refs_2_, ...), custom_call_target="tpu_custom_call" | custom-call | flops 2147483648 | bytes 7864356 | tf_op jit(solution)/shard_map/first/pallas_call | solution.py:20
  90.1 3.2 %second.9 = (bf16[256,512]{1,0:T(8,128)(2,1)S(1)}, bf16[256,512]{1,0:T(8,128)(2,1)S(1)}) custom-call(s32[9]{0:T(128)S(1)} %concatenate.3.info, bf16[256,512]{1,0:T(8,128)(2,1)S(1)} %get-tuple-element.41.refs_0_.refs_3_.refs_10_, bf16[256,512]{1,0:T(8,128)(2,1)S(1)} %collective-permute-done.17.refs_1_.refs_11_, ...), custom_call_target="tpu_custom_call" | custom-call | flops 1073741824 | bytes 9961508 | tf_op jit(solution)/shard_map/second/pallas_call | solution.py:20
  106.5 3.0 %collective-permute-start.31 = (f32[8,128]{1,0:T(8,128)S(1)}, f32[8,128]{1,0:T(8,128)S(1)}, u32[]{:S(2)}, u32[]{:S(2)}) collective-permute-start(f32[8,128]{1,0:T(8,128)S(1)} %add.79), channel_id=1, source_target_pairs={{0,16},{4,20},{8,24},{12,28},{16,0},{20,4},{24,8},{28,12},{1,17},{... | collective-permute-start | bytes 12296 | tf_op jit(solution)/shard_map/ppermute | solution.py:218
  115.2 5.5 %collective-permute-done.40.refs_2_ = bf16[256,512]{1,0:T(8,128)(2,1)S(1)} collective-permute-done((bf16[256,512]{1,0:T(8,128)(2,1)S(1)}, bf16[256,512]{1,0:T(8,128)(2,1)S(1)}, u32[]{:S(2)}, u32[]{:S(2)}) %collective-permute-start.40) | collective-permute-done | bytes 262176 | tf_op jit(solution)/shard_map/ppermute | solution.py:248
  120.8 3.5 %collective-permute-start.42 = (bf16[256,512]{1,0:T(8,128)(2,1)S(1)}, bf16[256,512]{1,0:T(8,128)(2,1)S(1)}, u32[]{:S(2)}, u32[]{:S(2)}) collective-permute-start(bf16[256,512]{1,0:T(8,128)(2,1)S(1)} %collective-permute-done.40.refs_2_), channel_id=1, source_target_pairs={{0,8},{8,16},{16,24},{12,4},{20,12},{28,20},{1,9},{9,17},{17,25},{... | collective-permute-start | bytes 786440 | tf_op jit(solution)/shard_map/ppermute | solution.py:249
  124.4 3.7 %collective-permute-start.38 = (bf16[256,512]{1,0:T(8,128)(2,1)S(1)}, bf16[256,512]{1,0:T(8,128)(2,1)S(1)}, u32[]{:S(2)}, u32[]{:S(2)}) collective-permute-start(bf16[256,512]{1,0:T(8,128)(2,1)S(1)} %collective-permute-done.36.refs_2_), channel_id=1, source_target_pairs={{0,8},{8,16},{16,24},{12,4},{20,12},{28,20},{1,9},{9,17},{17,25},{... | collective-permute-start | bytes 786440 | tf_op jit(solution)/shard_map/ppermute | solution.py:249
  129.2 4.9 %collective-permute-done.38.refs_4_ = bf16[256,512]{1,0:T(8,128)(2,1)S(1)} collective-permute-done((bf16[256,512]{1,0:T(8,128)(2,1)S(1)}, bf16[256,512]{1,0:T(8,128)(2,1)S(1)}, u32[]{:S(2)}, u32[]{:S(2)}) %collective-permute-start.38) | collective-permute-done | bytes 262176 | tf_op jit(solution)/shard_map/ppermute | solution.py:249
  134.1 4.0 %first.5.refs_8_ = f32[2,512,512]{2,1,0:T(8,128)S(1)} custom-call(s32[9]{0:T(128)S(1)} %concatenate.3.info, bf16[256,512]{1,0:T(8,128)(2,1)S(1)} %get-tuple-element.46.refs_0_.refs_4_, bf16[256,512]{1,0:T(8,128)(2,1)S(1)} %collective-permute-done.32.refs_1_.refs_5_, bf16[256,512]{1,0:T(8,128)(2,1)S(1)} %collective-permute-done.40.refs_2_, ...), custom_call_target="tpu_custom_call" | custom-call | flops 2147483648 | bytes 7864356 | tf_op jit(solution)/shard_map/first/pallas_call | solution.py:20
  138.1 3.2 %second.11 = (bf16[256,512]{1,0:T(8,128)(2,1)S(1)}, bf16[256,512]{1,0:T(8,128)(2,1)S(1)}) custom-call(s32[9]{0:T(128)S(1)} %concatenate.3.info, bf16[256,512]{1,0:T(8,128)(2,1)S(1)} %get-tuple-element.49.refs_0_.refs_4_.refs_12_, bf16[256,512]{1,0:T(8,128)(2,1)S(1)} %collective-permute-done.35.refs_1_.refs_13_, ...), custom_call_target="tpu_custom_call" | custom-call | flops 1073741824 | bytes 9961508 | tf_op jit(solution)/shard_map/second/pallas_call | solution.py:20
  156.3 2.8 %collective-permute-start.49 = (f32[8,128]{1,0:T(8,128)S(1)}, f32[8,128]{1,0:T(8,128)S(1)}, u32[]{:S(2)}, u32[]{:S(2)}) collective-permute-start(f32[8,128]{1,0:T(8,128)S(1)} %add.84), channel_id=1, source_target_pairs={{0,16},{4,20},{8,24},{12,28},{16,0},{20,4},{24,8},{28,12},{1,17},{... | collective-permute-start | bytes 12296 | tf_op jit(solution)/shard_map/ppermute | solution.py:218
  172.2 2.8 %collective-permute-start.57 = (f32[8,128]{1,0:T(8,128)S(1)}, f32[8,128]{1,0:T(8,128)S(1)}, u32[]{:S(2)}, u32[]{:S(2)}) collective-permute-start(f32[8,128]{1,0:T(8,128)S(1)} %add.89), channel_id=1, source_target_pairs={{0,16},{4,20},{8,24},{12,28},{16,0},{20,4},{24,8},{28,12},{1,17},{... | collective-permute-start | bytes 12296 | tf_op jit(solution)/shard_map/ppermute | solution.py:218
  176.7 3.9 %last.1 = (bf16[2,512,512]{2,1,0:T(8,128)(2,1)}, f32[2,3]{1,0:T(2,128)}) custom-call(s32[9]{0:T(128)S(1)} %concatenate.3.info, bf16[256,512]{1,0:T(8,128)(2,1)S(1)} %get-tuple-element.31.refs_0_.refs_2_, bf16[256,512]{1,0:T(8,128)(2,1)S(1)} %get-tuple-element.32.refs_1_, bf16[256,512]{1,0:T(8,128)(2,1)S(1)} %get-tuple-element.38.refs_0_.refs_3_.refs_2_, ...), custom_call_target="tpu_custom_call" | custom-call | bytes 4210724 | tf_op jit(solution)/shard_map/last/pallas_call | solution.py:20
  (147 shorter events, 84.8 us)
Async XLA Ops:
  6.0 10.1 %collective-permute-start.4 = (bf16[256,512]{1,0:T(8,128)(2,1)S(1)}, bf16[256,512]{1,0:T(8,128)(2,1)S(1)}, u32[]{:S(2)}, u32[]{:S(2)}) collective-permute-start(bf16[256,512]{1,0:T(8,128)(2,1)S(1)} %get-tuple-element.31.refs_0_.refs_2_), channel_id=1, source_target_pairs={{0,4},{4,0},{8,12},{12,8},{16,20},{20,16},{24,28},{28,24},{1,5},{5... | collective-permute-start | bytes 786440 | tf_op jit(solution)/shard_map/ppermute | solution.py:248
  9.0 11.9 %collective-permute-start = (bf16[256,512]{1,0:T(8,128)(2,1)S(1)}, bf16[256,512]{1,0:T(8,128)(2,1)S(1)}, u32[]{:S(2)}, u32[]{:S(2)}) collective-permute-start(bf16[256,512]{1,0:T(8,128)(2,1)S(1)} %get-tuple-element.33.refs_0_.refs_2_.refs_8_), channel_id=1, source_target_pairs={{0,4},{4,0},{8,12},{12,8},{16,20},{20,16},{24,28},{28,24},{1,5},{5... | collective-permute-start | bytes 786440 | tf_op jit(solution)/shard_map/ppermute | solution.py:248
  16.1 8.6 %collective-permute-start.6 = (bf16[256,512]{1,0:T(8,128)(2,1)S(1)}, bf16[256,512]{1,0:T(8,128)(2,1)S(1)}, u32[]{:S(2)}, u32[]{:S(2)}) collective-permute-start(bf16[256,512]{1,0:T(8,128)(2,1)S(1)} %collective-permute-done.4.refs_2_), channel_id=1, source_target_pairs={{0,8},{8,16},{16,24},{12,4},{20,12},{28,20},{1,9},{9,17},{17,25},{... | collective-permute-start | bytes 786440 | tf_op jit(solution)/shard_map/ppermute | solution.py:249
  20.9 8.7 %collective-permute-start.2 = (bf16[256,512]{1,0:T(8,128)(2,1)S(1)}, bf16[256,512]{1,0:T(8,128)(2,1)S(1)}, u32[]{:S(2)}, u32[]{:S(2)}) collective-permute-start(bf16[256,512]{1,0:T(8,128)(2,1)S(1)} %collective-permute-done.refs_2_), channel_id=1, source_target_pairs={{0,8},{8,16},{16,24},{12,4},{20,12},{28,20},{1,9},{9,17},{17,25},{... | collective-permute-start | bytes 786440 | tf_op jit(solution)/shard_map/ppermute | solution.py:249
  25.3 12.2 %collective-permute-start.1 = (bf16[256,512]{1,0:T(8,128)(2,1)S(1)}, bf16[256,512]{1,0:T(8,128)(2,1)S(1)}, u32[]{:S(2)}, u32[]{:S(2)}) collective-permute-start(bf16[256,512]{1,0:T(8,128)(2,1)S(1)} %collective-permute-done.refs_2_), channel_id=1, source_target_pairs={{0,1},{1,0},{2,3},{3,2},{4,5},{5,4},{6,7},{7,6},{8,9},{9,8},{10,11... | collective-permute-start | bytes 786440 | tf_op jit(solution)/shard_map/ppermute | solution.py:212
  29.7 7.8 %collective-permute-start.3 = (bf16[256,512]{1,0:T(8,128)(2,1)S(1)}, bf16[256,512]{1,0:T(8,128)(2,1)S(1)}, u32[]{:S(2)}, u32[]{:S(2)}) collective-permute-start(bf16[256,512]{1,0:T(8,128)(2,1)S(1)} %collective-permute-done.2.refs_4_), channel_id=1, source_target_pairs={{0,1},{1,0},{2,3},{3,2},{4,5},{5,4},{6,7},{7,6},{8,9},{9,8},{10,11... | collective-permute-start | bytes 786440 | tf_op jit(solution)/shard_map/ppermute | solution.py:212
  43.6 17.4 %collective-permute-start.9 = (bf16[256,512]{1,0:T(8,128)(2,1)S(1)}, bf16[256,512]{1,0:T(8,128)(2,1)S(1)}, u32[]{:S(2)}, u32[]{:S(2)}) collective-permute-start(bf16[256,512]{1,0:T(8,128)(2,1)S(1)} %add.91.refs_0_), channel_id=1, source_target_pairs={{0,2},{1,3},{2,0},{3,1},{4,6},{5,7},{6,4},{7,5},{8,10},{9,11},{10,... | collective-permute-start | bytes 786440 | tf_op jit(solution)/shard_map/ppermute | solution.py:269
  46.6 17.1 %collective-permute-start.16 = (bf16[256,512]{1,0:T(8,128)(2,1)S(1)}, bf16[256,512]{1,0:T(8,128)(2,1)S(1)}, u32[]{:S(2)}, u32[]{:S(2)}) collective-permute-start(bf16[256,512]{1,0:T(8,128)(2,1)S(1)} %add.92.refs_0_), channel_id=1, source_target_pairs={{0,2},{1,3},{2,0},{3,1},{4,6},{5,7},{6,4},{7,5},{8,10},{9,11},{10,... | collective-permute-start | bytes 786440 | tf_op jit(solution)/shard_map/ppermute | solution.py:269
  61.9 8.7 %collective-permute-start.22 = (bf16[256,512]{1,0:T(8,128)(2,1)S(1)}, bf16[256,512]{1,0:T(8,128)(2,1)S(1)}, u32[]{:S(2)}, u32[]{:S(2)}) collective-permute-start(bf16[256,512]{1,0:T(8,128)(2,1)S(1)} %get-tuple-element.38.refs_0_.refs_3_.refs_2_), channel_id=1, source_target_pairs={{0,4},{4,0},{8,12},{12,8},{16,20},{20,16},{24,28},{28,24},{1,5},{5... | collective-permute-start | bytes 786440 | tf_op jit(solution)/shard_map/ppermute | solution.py:248
  64.6 9.6 %collective-permute-start.18 = (bf16[256,512]{1,0:T(8,128)(2,1)S(1)}, bf16[256,512]{1,0:T(8,128)(2,1)S(1)}, u32[]{:S(2)}, u32[]{:S(2)}) collective-permute-start(bf16[256,512]{1,0:T(8,128)(2,1)S(1)} %get-tuple-element.41.refs_0_.refs_3_.refs_10_), channel_id=1, source_target_pairs={{0,4},{4,0},{8,12},{12,8},{16,20},{20,16},{24,28},{28,24},{1,5},{5... | collective-permute-start | bytes 786440 | tf_op jit(solution)/shard_map/ppermute | solution.py:248
  74.2 9.7 %collective-permute-start.20 = (bf16[256,512]{1,0:T(8,128)(2,1)S(1)}, bf16[256,512]{1,0:T(8,128)(2,1)S(1)}, u32[]{:S(2)}, u32[]{:S(2)}) collective-permute-start(bf16[256,512]{1,0:T(8,128)(2,1)S(1)} %collective-permute-done.18.refs_2_), channel_id=1, source_target_pairs={{0,8},{8,16},{16,24},{12,4},{20,12},{28,20},{1,9},{9,17},{17,25},{... | collective-permute-start | bytes 786440 | tf_op jit(solution)/shard_map/ppermute | solution.py:249
  78.3 9.6 %collective-permute-start.17 = (bf16[256,512]{1,0:T(8,128)(2,1)S(1)}, bf16[256,512]{1,0:T(8,128)(2,1)S(1)}, u32[]{:S(2)}, u32[]{:S(2)}) collective-permute-start(bf16[256,512]{1,0:T(8,128)(2,1)S(1)} %get-tuple-element.41.refs_0_.refs_3_.refs_10_), channel_id=1, source_target_pairs={{0,1},{1,0},{2,3},{3,2},{4,5},{5,4},{6,7},{7,6},{8,9},{9,8},{10,11... | collective-permute-start | bytes 786440 | tf_op jit(solution)/shard_map/ppermute | solution.py:212
  78.5 9.4 %collective-permute-start.19 = (bf16[256,512]{1,0:T(8,128)(2,1)S(1)}, bf16[256,512]{1,0:T(8,128)(2,1)S(1)}, u32[]{:S(2)}, u32[]{:S(2)}) collective-permute-start(bf16[256,512]{1,0:T(8,128)(2,1)S(1)} %collective-permute-done.18.refs_2_), channel_id=1, source_target_pairs={{0,1},{1,0},{2,3},{3,2},{4,5},{5,4},{6,7},{7,6},{8,9},{9,8},{10,11... | collective-permute-start | bytes 786440 | tf_op jit(solution)/shard_map/ppermute | solution.py:212
  94.0 17.1 %collective-permute-start.27 = (bf16[256,512]{1,0:T(8,128)(2,1)S(1)}, bf16[256,512]{1,0:T(8,128)(2,1)S(1)}, u32[]{:S(2)}, u32[]{:S(2)}) collective-permute-start(bf16[256,512]{1,0:T(8,128)(2,1)S(1)} %add.93.refs_0_), channel_id=1, source_target_pairs={{0,2},{1,3},{2,0},{3,1},{4,6},{5,7},{6,4},{7,5},{8,10},{9,11},{10,... | collective-permute-start | bytes 786440 | tf_op jit(solution)/shard_map/ppermute | solution.py:269
  96.7 17.0 %collective-permute-start.34 = (bf16[256,512]{1,0:T(8,128)(2,1)S(1)}, bf16[256,512]{1,0:T(8,128)(2,1)S(1)}, u32[]{:S(2)}, u32[]{:S(2)}) collective-permute-start(bf16[256,512]{1,0:T(8,128)(2,1)S(1)} %add.94.refs_0_), channel_id=1, source_target_pairs={{0,2},{1,3},{2,0},{3,1},{4,6},{5,7},{6,4},{7,5},{8,10},{9,11},{10,... | collective-permute-start | bytes 786440 | tf_op jit(solution)/shard_map/ppermute | solution.py:269
  112.1 8.7 %collective-permute-start.40 = (bf16[256,512]{1,0:T(8,128)(2,1)S(1)}, bf16[256,512]{1,0:T(8,128)(2,1)S(1)}, u32[]{:S(2)}, u32[]{:S(2)}) collective-permute-start(bf16[256,512]{1,0:T(8,128)(2,1)S(1)} %get-tuple-element.46.refs_0_.refs_4_), channel_id=1, source_target_pairs={{0,4},{4,0},{8,12},{12,8},{16,20},{20,16},{24,28},{28,24},{1,5},{5... | collective-permute-start | bytes 786440 | tf_op jit(solution)/shard_map/ppermute | solution.py:248
  114.7 9.7 %collective-permute-start.36 = (bf16[256,512]{1,0:T(8,128)(2,1)S(1)}, bf16[256,512]{1,0:T(8,128)(2,1)S(1)}, u32[]{:S(2)}, u32[]{:S(2)}) collective-permute-start(bf16[256,512]{1,0:T(8,128)(2,1)S(1)} %get-tuple-element.49.refs_0_.refs_4_.refs_12_), channel_id=1, source_target_pairs={{0,4},{4,0},{8,12},{12,8},{16,20},{20,16},{24,28},{28,24},{1,5},{5... | collective-permute-start | bytes 786440 | tf_op jit(solution)/shard_map/ppermute | solution.py:248
  124.4 9.7 %collective-permute-start.38 = (bf16[256,512]{1,0:T(8,128)(2,1)S(1)}, bf16[256,512]{1,0:T(8,128)(2,1)S(1)}, u32[]{:S(2)}, u32[]{:S(2)}) collective-permute-start(bf16[256,512]{1,0:T(8,128)(2,1)S(1)} %collective-permute-done.36.refs_2_), channel_id=1, source_target_pairs={{0,8},{8,16},{16,24},{12,4},{20,12},{28,20},{1,9},{9,17},{17,25},{... | collective-permute-start | bytes 786440 | tf_op jit(solution)/shard_map/ppermute | solution.py:249
  128.6 9.5 %collective-permute-start.35 = (bf16[256,512]{1,0:T(8,128)(2,1)S(1)}, bf16[256,512]{1,0:T(8,128)(2,1)S(1)}, u32[]{:S(2)}, u32[]{:S(2)}) collective-permute-start(bf16[256,512]{1,0:T(8,128)(2,1)S(1)} %get-tuple-element.49.refs_0_.refs_4_.refs_12_), channel_id=1, source_target_pairs={{0,1},{1,0},{2,3},{3,2},{4,5},{5,4},{6,7},{7,6},{8,9},{9,8},{10,11... | collective-permute-start | bytes 786440 | tf_op jit(solution)/shard_map/ppermute | solution.py:212
  128.8 9.3 %collective-permute-start.37 = (bf16[256,512]{1,0:T(8,128)(2,1)S(1)}, bf16[256,512]{1,0:T(8,128)(2,1)S(1)}, u32[]{:S(2)}, u32[]{:S(2)}) collective-permute-start(bf16[256,512]{1,0:T(8,128)(2,1)S(1)} %collective-permute-done.36.refs_2_), channel_id=1, source_target_pairs={{0,1},{1,0},{2,3},{3,2},{4,5},{5,4},{6,7},{7,6},{8,9},{9,8},{10,11... | collective-permute-start | bytes 786440 | tf_op jit(solution)/shard_map/ppermute | solution.py:212
  144.2 16.6 %collective-permute-start.52 = (bf16[256,512]{1,0:T(8,128)(2,1)S(1)}, bf16[256,512]{1,0:T(8,128)(2,1)S(1)}, u32[]{:S(2)}, u32[]{:S(2)}) collective-permute-start(bf16[256,512]{1,0:T(8,128)(2,1)S(1)} %add.96.refs_0_), channel_id=1, source_target_pairs={{0,2},{1,3},{2,0},{3,1},{4,6},{5,7},{6,4},{7,5},{8,10},{9,11},{10,... | collective-permute-start | bytes 786440 | tf_op jit(solution)/shard_map/ppermute | solution.py:269
  146.9 15.2 %collective-permute-start.45 = (bf16[256,512]{1,0:T(8,128)(2,1)S(1)}, bf16[256,512]{1,0:T(8,128)(2,1)S(1)}, u32[]{:S(2)}, u32[]{:S(2)}) collective-permute-start(bf16[256,512]{1,0:T(8,128)(2,1)S(1)} %add.95.refs_0_), channel_id=1, source_target_pairs={{0,2},{1,3},{2,0},{3,1},{4,6},{5,7},{6,4},{7,5},{8,10},{9,11},{10,... | collective-permute-start | bytes 786440 | tf_op jit(solution)/shard_map/ppermute | solution.py:269
  162.0 14.7 %collective-permute-start.53 = (bf16[256,512]{1,0:T(8,128)(2,1)S(1)}, bf16[256,512]{1,0:T(8,128)(2,1)S(1)}, u32[]{:S(2)}, u32[]{:S(2)}) collective-permute-start(bf16[256,512]{1,0:T(8,128)(2,1)S(1)} %get-tuple-element.57.refs_14_), channel_id=1, source_target_pairs={{0,1},{1,0},{2,3},{3,2},{4,5},{5,4},{6,7},{7,6},{8,9},{9,8},{10,11... | collective-permute-start | bytes 786440 | tf_op jit(solution)/shard_map/ppermute | solution.py:212
  163.2 13.5 %collective-permute-start.50 = (bf16[256,512]{1,0:T(8,128)(2,1)S(1)}, bf16[256,512]{1,0:T(8,128)(2,1)S(1)}, u32[]{:S(2)}, u32[]{:S(2)}) collective-permute-start(bf16[256,512]{1,0:T(8,128)(2,1)S(1)} %get-tuple-element.54.refs_6_), channel_id=1, source_target_pairs={{0,1},{1,0},{2,3},{3,2},{4,5},{5,4},{6,7},{7,6},{8,9},{9,8},{10,11... | collective-permute-start | bytes 786440 | tf_op jit(solution)/shard_map/ppermute | solution.py:212
  (39 other events, 150.8 us)

commit v2 on v1

v2 whole, which is shorter than its diff:
```python
import functools

import jax
import jax.numpy as jnp
from jax import lax
from jax.experimental import pallas as pl
from jax.experimental.pallas import tpu as pltpu
from jax.sharding import PartitionSpec as P

PRODUCTS = 3
F32 = jnp.float32
BF16 = jnp.bfloat16
VMEM = pl.BlockSpec(memory_space=pltpu.VMEM)
SMEM = pl.BlockSpec(memory_space=pltpu.SMEM)


class Info:
    def __init__(self, shifts_ref, rows_ref, sectors):
        self.core = lax.axis_index("op") % 2
        self.sec = lax.axis_index("sec")
        self.shift = lambda w: shifts_ref[w]
        self.rows = lambda t: rows_ref[self.sec * sectors + t]
        self.live = lambda: sum(rows_ref[i] for i in range(rows_ref.shape[0])).astype(F32)

    def part(self, which, half):
        return pl.ds(pl.multiple_of((self.core if which == 0 else 1 - self.core) * half, half), half)


def after(value, *others):
    return lax.optimization_barrier((value, *others))[0]


def call(kernel, name, out, scratch, *operands, flops=0):
    moved = sum(a.size * a.dtype.itemsize for a in operands)
    return pl.pallas_call(
        kernel,
        name=name,
        out_shape=out,
        in_specs=[SMEM, SMEM] + [VMEM] * (len(operands) - 2),
        out_specs=jax.tree.map(lambda _: VMEM, out),
        scratch_shapes=scratch,
        compiler_params=pltpu.CompilerParams(vmem_limit_bytes=24 << 20),
        cost_estimate=pl.CostEstimate(flops=flops, bytes_accessed=moved, transcendentals=0),
    )(*operands)


def lane_sums(value):
    rows, columns = value.shape
    folded = sum(value[:, i : i + 128] for i in range(0, columns, 128))
    return jnp.sum(folded, axis=0, keepdims=True)


def total(stats_ref, row, live):
    return jnp.sum(stats_ref[row : row + 1, :], axis=1, keepdims=True) / live


def write_sums(stats_ref, values):
    rows = stats_ref.shape[0]
    parts = [lane_sums(v) for v in values]
    parts += [jnp.zeros((1, 128), F32)] * (rows - len(parts))
    stats_ref[...] = jnp.concatenate(parts, axis=0)


def coefficients(stats, live):
    norm = jnp.sqrt(total(stats[0], 0, live))
    alphas, betas = [], []
    for k, ref in enumerate(stats[1:]):
        alpha = total(ref, 1, live)
        square = total(ref, 0, live) - alpha * alpha
        if k:
            square = square - 2.0 * betas[-1] * total(ref, 2, live) + betas[-1] * betas[-1]
        alphas.append(alpha)
        betas.append(jnp.sqrt(jnp.maximum(square, 0.0)))
    return norm, alphas, betas


def lanczos_vectors(norm, alphas, betas):
    vectors = [[1.0 / norm]]
    for k, beta in enumerate(betas):
        scale = 1.0 / beta
        one = [-alphas[k] * c for c in vectors[k]] + [1.0]
        if k:
            for i, c in enumerate(vectors[k - 1]):
                one[i] = one[i] - betas[k - 1] * c
        vectors.append([c * scale for c in one])
    return vectors


def combine(coefs, blocks):
    return sum(c * block for c, block in zip(coefs, blocks))


def start_kernel(shifts_ref, rows_ref, x_ref, *refs):
    *halves, stats_ref = refs
    sectors, block_rows, _ = x_ref.shape
    half = block_rows // 2
    info = Info(shifts_ref, rows_ref, sectors)
    square = 0.0
    for t in range(sectors):
        for which in range(2):
            part = info.part(which, half)
            value = x_ref[t, part, :]
            rows = lax.broadcasted_iota(jnp.int32, value.shape, 0) + part.start
            value = jnp.where(rows < info.rows(t), value, jnp.zeros_like(value))
            halves[2 * t + which][...] = value
            if which == 0:
                wide = value.astype(F32)
                square = square + wide * wide
    write_sums(stats_ref, [square])


def select_source(info, block, refs, v_ref):
    half = refs[0].shape[0]
    even = info.sec % 2 == 0
    mine, other = info.part(0, half), info.part(1, half)
    from_pair = (block == 1) == even
    for k, here in enumerate(
        (block == 0, (block != 0) & from_pair, (block != 0) & jnp.logical_not(from_pair))
    ):

        @pl.when(here)
        def _():
            v_ref[mine, :] = refs[2 * k][...]
            v_ref[other, :] = refs[2 * k + 1][...]


def apply_term(info, w, target, refs, left_ref, right_ref, v_ref, acc_ref):
    select_source(info, (target - info.shift(w)) >> 1, refs, v_ref)
    part = jnp.dot(v_ref[...], right_ref[w], preferred_element_type=F32).astype(BF16)
    acc_ref[...] += jnp.dot(left_ref[w, target], part, preferred_element_type=F32)


def first_kernel(shifts_ref, rows_ref, *refs):
    *sources, left_ref, right_ref, acc_ref, v_ref = refs
    info = Info(shifts_ref, rows_ref, left_ref.shape[1])
    acc_ref[...] = jnp.zeros_like(acc_ref)

    def step(w, carry):
        target = info.shift(w) & 1
        apply_term(info, w, target, sources, left_ref, right_ref, v_ref, acc_ref.at[target])
        return carry

    lax.fori_loop(0, left_ref.shape[0], step, 0)


def second_kernel(target, shifts_ref, rows_ref, *refs):
    *sources, left_ref, right_ref, sum_ref, mine_ref, other_ref, v_ref, acc_ref = refs
    half = mine_ref.shape[0]
    info = Info(shifts_ref, rows_ref, left_ref.shape[1])
    acc_ref[...] = sum_ref[target]

    def step(w, carry):
        @pl.when(((info.shift(w) + 1) & 1) == target)
        def _():
            apply_term(info, w, target, sources, left_ref, right_ref, v_ref, acc_ref)

        return carry

    lax.fori_loop(0, left_ref.shape[0], step, 0)
    mine_ref[...] = acc_ref[info.part(0, half), :].astype(BF16)
    other_ref[...] = acc_ref[info.part(1, half), :].astype(BF16)


def add_kernel(shifts_ref, rows_ref, a_ref, b_ref, out_ref):
    out_ref[...] = (a_ref[...].astype(F32) + b_ref[...].astype(F32)).astype(BF16)


def image_kernel(product, target, sectors, shifts_ref, rows_ref, *refs):
    a_ref, b_ref = refs[:2]
    basis = [r[...].astype(F32) for r in refs[2 : 3 + product]]
    stats = refs[3 + product : 4 + 2 * product]
    out_ref, stats_ref = refs[4 + 2 * product :]
    half, columns = out_ref.shape
    info = Info(shifts_ref, rows_ref, sectors)
    live = info.live() * columns
    norm, alphas, betas = coefficients(stats, live)
    vectors = [combine(c, basis) for c in lanczos_vectors(norm, alphas, betas)[-2:]]
    value = a_ref[...].astype(F32) + b_ref[...].astype(F32)
    if product == 0:
        value = value * (1.0 / norm)
    else:
        value = value - alphas[-1] * basis[-1]
        if product > 1:
            value = value - betas[-2] * basis[-2]
        value = value * (1.0 / betas[-1])
    rows = lax.broadcasted_iota(jnp.int32, value.shape, 0) + info.core * half
    value = jnp.where(rows < info.rows(target), value, 0.0).astype(BF16)
    out_ref[...] = value
    value = value.astype(F32)
    write_sums(stats_ref, [value * value] + [value * v for v in vectors[::-1]])


def last_kernel(products, shifts_ref, rows_ref, *refs):
    per_sector = 2 * (products + 1)
    stats = refs[-3 - products : -2]
    out_ref, coef_ref = refs[-2:]
    sectors, block_rows, columns = out_ref.shape
    half = block_rows // 2
    info = Info(shifts_ref, rows_ref, sectors)
    norm, alphas, betas = coefficients(stats, info.live() * columns)
    coefs = lanczos_vectors(norm, alphas, betas)[-1]
    for t in range(sectors):
        for which in range(2):
            basis = [
                refs[t * per_sector + 2 * k + which][...].astype(F32) for k in range(products + 1)
            ]
            out_ref[t, info.part(which, half), :] = combine(coefs, basis).astype(BF16)
    row = lax.broadcasted_iota(jnp.int32, coef_ref.shape, 0)
    column = lax.broadcasted_iota(jnp.int32, coef_ref.shape, 1)
    value = jnp.zeros(coef_ref.shape, F32)
    for k in range(products):
        value = jnp.where((row == 0) & (column == k), alphas[k], value)
        value = jnp.where((row == 1) & (column == k), betas[k], value)
    coef_ref[...] = value


def on_device(wavefunction, left_blocks, right_blocks, charge_shifts, sector_rows):
    sectors, block_rows, columns = wavefunction.shape
    half = block_rows // 2
    n_sec, n_op = lax.axis_size("sec"), lax.axis_size("op")
    assert sectors == 2 and n_sec % 2 == 0 and n_op % 2 == 0
    core_pairs = [(i, i ^ 1) for i in range(n_op)]
    pairs = [(i, i ^ 1) for i in range(n_sec)]
    onward = [(i, i + 2) for i in range(0, n_sec - 2, 2)]
    onward += [(i, i - 2) for i in range(3, n_sec, 2)]

    def across_cores(value):
        return lax.ppermute(value, "op", core_pairs)

    def sum_steps(stats):
        stats = stats + across_cores(stats)
        bit = 1
        while bit < n_sec:
            stats = stats + lax.ppermute(stats, "sec", [(i, i ^ bit) for i in range(n_sec)])
            yield stats
            bit *= 2

    place = (charge_shifts, sector_rows)
    half_type = jax.ShapeDtypeStruct((half, columns), BF16)
    stats_type = jax.ShapeDtypeStruct((8, 128), F32)
    acc_type = jax.ShapeDtypeStruct((sectors, block_rows, columns), F32)
    v_scratch = pltpu.VMEM((block_rows, columns), BF16)
    acc_scratch = pltpu.VMEM((block_rows, columns), F32)

    *halves, start_stats = call(
        start_kernel, "start", [half_type] * (2 * sectors) + [stats_type], [], *place, wavefunction
    )
    basis = [[(halves[0], halves[1]), (halves[2], halves[3])]]
    stats = []
    sums = start_stats
    pair_flops = 4 * block_rows * block_rows * columns
    terms = left_blocks.shape[0]

    for product in range(PRODUCTS):
        steps = list(sum_steps(sums))
        stats.append(steps[-1])
        (mine_0, other_0), (mine_1, other_1) = basis[-1]
        pair_0 = lax.ppermute(mine_0, "sec", pairs)
        pair_1 = lax.ppermute(mine_1, "sec", pairs)
        pair_0 = after(pair_0, steps[0])
        far_0 = lax.ppermute(pair_0, "sec", onward)
        if len(steps) > 1:
            pair_1 = after(pair_1, steps[1])
        far_1 = lax.ppermute(pair_1, "sec", onward)
        acc = call(
            first_kernel, "first", acc_type, [v_scratch], *place,
            mine_0, other_0, pair_0, across_cores(pair_0), far_0, across_cores(far_0),
            left_blocks, right_blocks, flops=terms * pair_flops,
        )
        far_1 = after(far_1, acc)
        sources = (mine_1, other_1, pair_1, across_cores(pair_1), far_1, across_cores(far_1))
        image = []
        sums = []
        for t in range(sectors):
            mine, other = call(
                functools.partial(second_kernel, t), "second", [half_type] * 2,
                [v_scratch, acc_scratch], *place,
                *sources, left_blocks, right_blocks, acc, flops=terms * pair_flops // 2,
            )
            value = call(add_kernel, "add", half_type, [], *place, mine, across_cores(other))
            bit = 2
            while 2 * bit < n_op:
                arrived = lax.ppermute(value, "op", [(i, i ^ bit) for i in range(n_op)])
                value = call(add_kernel, "add", half_type, [], *place, value, arrived)
                bit *= 2
            arrived = lax.ppermute(value, "op", [(i, i ^ bit) for i in range(n_op)])
            mine, part = call(
                functools.partial(image_kernel, product, t, sectors), "image",
                [half_type, stats_type], [], *place,
                value, arrived, *[b[t][0] for b in basis], *stats,
            )
            image.append((mine, across_cores(mine)))
            sums.append(part)
        basis.append(image)
        sums = sums[0] + sums[1]
    stats.append(list(sum_steps(sums))[-1])

    flat = [h for t in range(sectors) for b in basis for h in b[t]]
    vector_type = jax.ShapeDtypeStruct(wavefunction.shape, BF16)
    coef_type = jax.ShapeDtypeStruct((2, PRODUCTS), F32)
    vector, coef = call(
        functools.partial(last_kernel, PRODUCTS), "last", [vector_type, coef_type], [],
        *place, *flat, *stats,
    )
    return vector, coef


def solution(mesh):
    in_specs = (P("sec", None, None), P("op", "sec", None, None), P("op", None, None), P("op"), P())
    out_specs = (P("sec", None, None), P())
    return jax.shard_map(
        on_device, mesh=mesh, in_specs=in_specs, out_specs=out_specs, check_vma=False
    )
```

time: 183 us -> 180 us (0.984)
  waiting for transfers between devices: 58 us -> 63.2 us
  starting transfers between devices: 72.4 us -> 67.6 us
    ppermute x6, waiting for transfers between devices: 0.02 us -> 14.5 us  [on_device(): arrived = lax.ppermute(value, 'op', [(i, i ^ bit) for i in range(n_op)])]
    ppermute x24, waiting for transfers between devices: 53.5 us -> 40 us  [the longest x12 26.6 us: sum_steps(): lax.ppermute(stats, 'sec', [(i, i ^ bit) for i in range(n_sec)])]
    ppermute x24, starting transfers between devices: 57.7 us -> 53.1 us  [the longest x12 25 us: sum_steps(): lax.ppermute(stats, 'sec', [(i, i ^ bit) for i in range(n_sec)])]
    ppermute x28, waiting for transfers between devices: 4.55 us -> 8.76 us  [across_cores(): return lax.ppermute(value, 'op', core_pairs)]
    ppermute x6, starting transfers between devices: 8.95 us -> 6.78 us  [on_device(): arrived = lax.ppermute(value, 'op', [(i, i ^ bit) for i in range(n_op)])]
    ppermute x28, starting transfers between devices: 5.7 us -> 7.74 us  [across_cores(): return lax.ppermute(value, 'op', core_pairs)]
    unnamed x10 -> x14, local copies, waits for them, and re-layouts: 5.01 us -> 6.31 us
  transfers between devices with their start and end apart: 58 -> 58, of which waited for: 23 -> 30; matrix products, arithmetic and copies ran while one was open for 0% -> 0% of each run, Pallas kernels for 16% -> 16%
where the time goes in v2:
time: 180 us; the launch traced here: 178 us
  starting transfers between devices  67.6 us (38%)
  waiting for transfers between devices  63.2 us (35%)
  Pallas kernels  39.8 us (22%)
  local copies, waits for them, and re-layouts  6.31 us (4%)
    pallas_call x23, Pallas kernels, call(): pl.pallas_call(kernel, name=name, out_shape=out, in_specs=[SMEM, SMEM] +...  39.8 us
    ppermute x12, waiting for transfers between devices, sum_steps(): lax.ppermute(stats, 'sec', [(i, i ^ bit) for i in range(n_sec)])  26.6 us
    ppermute x12, starting transfers between devices, sum_steps(): lax.ppermute(stats, 'sec', [(i, i ^ bit) for i in range(n_sec)])  25 us
    ppermute x6, waiting for transfers between devices, on_device(): arrived = lax.ppermute(value, 'op', [(i, i ^ bit) for i in range(n_op)])  14.5 us
    ppermute x3, waiting for transfers between devices, on_device(): far_0 = lax.ppermute(pair_0, 'sec', onward)  12.6 us
    ppermute x3, starting transfers between devices, on_device(): far_1 = lax.ppermute(pair_1, 'sec', onward)  12 us
    ppermute x3, starting transfers between devices, on_device(): far_0 = lax.ppermute(pair_0, 'sec', onward)  11.6 us
    ppermute x28, waiting for transfers between devices, across_cores(): return lax.ppermute(value, 'op', core_pairs)  8.76 us
  transfers between devices with their start and end apart: 58, of which 30 were waited for; matrix products, arithmetic and copies ran while one was open for 0% of the time, Pallas kernels for 16%

profile of v2, /device:TPU:0, one launch (start us, length us, event | category | flops | bytes accessed | tf_op | source)
XLA Modules:
  0.0 178.1 jit_solution(7703519705390914925)
XLA Ops:
  3.9 3.0 %collective-permute-start.6 = (bf16[256,512]{1,0:T(8,128)(2,1)S(1)}, bf16[256,512]{1,0:T(8,128)(2,1)S(1)}, u32[]{:S(2)}, u32[]{:S(2)}) collective-permute-start(bf16[256,512]{1,0:T(8,128)(2,1)S(1)} %get-tuple-element.40.refs_0_.refs_2_), channel_id=1, source_target_pairs={{0,4},{4,0},{8,12},{12,8},{16,20},{20,16},{24,28},{28,24},{1,5},{5... | collective-permute-start | bytes 786440 | tf_op jit(solution)/shard_map/ppermute | solution.py:258
  8.2 5.1 %collective-permute-done.2 = f32[8,128]{1,0:T(8,128)S(1)} collective-permute-done((f32[8,128]{1,0:T(8,128)S(1)}, f32[8,128]{1,0:T(8,128)S(1)}, u32[]{:S(2)}, u32[]{:S(2)}) %collective-permute-start.2) | collective-permute-done | bytes 4128 | tf_op jit(solution)/shard_map/ppermute | solution.py:234
  13.3 3.7 %collective-permute-start.8 = (bf16[256,512]{1,0:T(8,128)(2,1)S(1)}, bf16[256,512]{1,0:T(8,128)(2,1)S(1)}, u32[]{:S(2)}, u32[]{:S(2)}) collective-permute-start(bf16[256,512]{1,0:T(8,128)(2,1)S(1)} %collective-permute-done.6.refs_2_), channel_id=1, source_target_pairs={{0,8},{8,16},{16,24},{12,4},{20,12},{28,20},{1,9},{9,17},{17,25},{... | collective-permute-start | bytes 786440 | tf_op jit(solution)/shard_map/ppermute | solution.py:261
  17.2 4.5 %collective-permute-done.8.refs_4_ = bf16[256,512]{1,0:T(8,128)(2,1)S(1)} collective-permute-done((bf16[256,512]{1,0:T(8,128)(2,1)S(1)}, bf16[256,512]{1,0:T(8,128)(2,1)S(1)}, u32[]{:S(2)}, u32[]{:S(2)}) %collective-permute-start.8) | collective-permute-done | bytes 262176 | tf_op jit(solution)/shard_map/ppermute | solution.py:261
  21.7 2.5 %collective-permute-start.3 = (f32[8,128]{1,0:T(8,128)S(1)}, f32[8,128]{1,0:T(8,128)S(1)}, u32[]{:S(2)}, u32[]{:S(2)}) collective-permute-start(f32[8,128]{1,0:T(8,128)S(1)} %add.64), channel_id=1, source_target_pairs={{0,8},{4,12},{8,0},{12,4},{16,24},{20,28},{24,16},{28,20},{1,9},{5... | collective-permute-start | bytes 12296 | tf_op jit(solution)/shard_map/ppermute | solution.py:234
  25.8 3.9 %collective-permute-start.5 = (bf16[256,512]{1,0:T(8,128)(2,1)S(1)}, bf16[256,512]{1,0:T(8,128)(2,1)S(1)}, u32[]{:S(2)}, u32[]{:S(2)}) collective-permute-start(bf16[256,512]{1,0:T(8,128)(2,1)S(1)} %collective-permute-done.refs_2_), channel_id=1, source_target_pairs={{0,8},{8,16},{16,24},{12,4},{20,12},{28,20},{1,9},{9,17},{17,25},{... | collective-permute-start | bytes 786440 | tf_op jit(solution)/shard_map/ppermute | solution.py:264
  33.6 4.0 %first.3.refs_8_ = f32[2,512,512]{2,1,0:T(8,128)S(1)} custom-call(s32[4]{0:T(128)S(1)} %copy-done.5, s32[16]{0:T(128)S(1)} %copy-done.6, bf16[256,512]{1,0:T(8,128)(2,1)S(1)} %get-tuple-element.40.refs_0_.refs_2_, bf16[256,512]{1,0:T(8,128)(2,1)S(1)} %get-tuple-element.41.refs_1_, bf16[256,512]{1,0:T(8,128)(2,1)S(1)} %collective-permute-done.6.refs_2_, ...), custom_call_target="tpu_custom_call" | custom-call | flops 2147483648 | bytes 7864400 | tf_op jit(solution)/shard_map/first/pallas_call | solution.py:35
  49.0 2.6 %collective-permute-start.13 = (f32[8,128]{1,0:T(8,128)S(1)}, f32[8,128]{1,0:T(8,128)S(1)}, u32[]{:S(2)}, u32[]{:S(2)}) collective-permute-start(f32[8,128]{1,0:T(8,128)S(1)} %add.65), channel_id=1, source_target_pairs={{0,16},{4,20},{8,24},{12,28},{16,0},{20,4},{24,8},{28,12},{1,17},{... | collective-permute-start | bytes 12296 | tf_op jit(solution)/shard_map/ppermute | solution.py:234
  56.4 3.8 %collective-permute-done.16.refs_1_ = bf16[256,512]{1,0:T(8,128)(2,1)S(1)} collective-permute-done((bf16[256,512]{1,0:T(8,128)(2,1)S(1)}, bf16[256,512]{1,0:T(8,128)(2,1)S(1)}, u32[]{:S(2)}, u32[]{:S(2)}) %collective-permute-start.16) | collective-permute-done | bytes 262176 | tf_op jit(solution)/shard_map/ppermute | solution.py:286
  62.2 3.6 %collective-permute-done.20 = f32[8,128]{1,0:T(8,128)S(1)} collective-permute-done((f32[8,128]{1,0:T(8,128)S(1)}, f32[8,128]{1,0:T(8,128)S(1)}, u32[]{:S(2)}, u32[]{:S(2)}) %collective-permute-start.20) | collective-permute-done | bytes 4128 | tf_op jit(solution)/shard_map/ppermute | solution.py:234
  65.9 3.5 %collective-permute-start.26 = (bf16[256,512]{1,0:T(8,128)(2,1)S(1)}, bf16[256,512]{1,0:T(8,128)(2,1)S(1)}, u32[]{:S(2)}, u32[]{:S(2)}) collective-permute-start(bf16[256,512]{1,0:T(8,128)(2,1)S(1)} %collective-permute-done.24.refs_2_), channel_id=1, source_target_pairs={{0,8},{8,16},{16,24},{12,4},{20,12},{28,20},{1,9},{9,17},{17,25},{... | collective-permute-start | bytes 786440 | tf_op jit(solution)/shard_map/ppermute | solution.py:261
  70.0 4.1 %collective-permute-done.26.refs_4_ = bf16[256,512]{1,0:T(8,128)(2,1)S(1)} collective-permute-done((bf16[256,512]{1,0:T(8,128)(2,1)S(1)}, bf16[256,512]{1,0:T(8,128)(2,1)S(1)}, u32[]{:S(2)}, u32[]{:S(2)}) %collective-permute-start.26) | collective-permute-done | bytes 262176 | tf_op jit(solution)/shard_map/ppermute | solution.py:261
  74.1 2.5 %collective-permute-start.21 = (f32[8,128]{1,0:T(8,128)S(1)}, f32[8,128]{1,0:T(8,128)S(1)}, u32[]{:S(2)}, u32[]{:S(2)}) collective-permute-start(f32[8,128]{1,0:T(8,128)S(1)} %add.69), channel_id=1, source_target_pairs={{0,8},{4,12},{8,0},{12,4},{16,24},{20,28},{24,16},{28,20},{1,9},{5... | collective-permute-start | bytes 12296 | tf_op jit(solution)/shard_map/ppermute | solution.py:234
  78.1 3.9 %collective-permute-start.23 = (bf16[256,512]{1,0:T(8,128)(2,1)S(1)}, bf16[256,512]{1,0:T(8,128)(2,1)S(1)}, u32[]{:S(2)}, u32[]{:S(2)}) collective-permute-start(bf16[256,512]{1,0:T(8,128)(2,1)S(1)} %collective-permute-done.18.refs_2_), channel_id=1, source_target_pairs={{0,8},{8,16},{16,24},{12,4},{20,12},{28,20},{1,9},{9,17},{17,25},{... | collective-permute-start | bytes 786440 | tf_op jit(solution)/shard_map/ppermute | solution.py:264
  82.7 4.0 %first.4.refs_8_ = f32[2,512,512]{2,1,0:T(8,128)S(1)} custom-call(s32[4]{0:T(128)S(1)} %copy-done.5, s32[16]{0:T(128)S(1)} %copy-done.6, bf16[256,512]{1,0:T(8,128)(2,1)S(1)} %get-tuple-element.50.refs_0_.refs_3_.refs_2_, bf16[256,512]{1,0:T(8,128)(2,1)S(1)} %collective-permute-done.14.refs_1_.refs_3_, bf16[256,512]{1,0:T(8,128)(2,1)S(1)} %collective-permute-done.24.refs_2_, ...), custom_call_target="tpu_custom_call" | custom-call | flops 2147483648 | bytes 7864400 | tf_op jit(solution)/shard_map/first/pallas_call | solution.py:35
  98.3 3.5 %collective-permute-start.31 = (f32[8,128]{1,0:T(8,128)S(1)}, f32[8,128]{1,0:T(8,128)S(1)}, u32[]{:S(2)}, u32[]{:S(2)}) collective-permute-start(f32[8,128]{1,0:T(8,128)S(1)} %add.70), channel_id=1, source_target_pairs={{0,16},{4,20},{8,24},{12,28},{16,0},{20,4},{24,8},{28,12},{1,17},{... | collective-permute-start | bytes 12296 | tf_op jit(solution)/shard_map/ppermute | solution.py:234
  115.3 4.4 %collective-permute-start.44 = (bf16[256,512]{1,0:T(8,128)(2,1)S(1)}, bf16[256,512]{1,0:T(8,128)(2,1)S(1)}, u32[]{:S(2)}, u32[]{:S(2)}) collective-permute-start(bf16[256,512]{1,0:T(8,128)(2,1)S(1)} %collective-permute-done.42.refs_2_), channel_id=1, source_target_pairs={{0,8},{8,16},{16,24},{12,4},{20,12},{28,20},{1,9},{9,17},{17,25},{... | collective-permute-start | bytes 786440 | tf_op jit(solution)/shard_map/ppermute | solution.py:261
  120.3 4.1 %collective-permute-done.44.refs_4_ = bf16[256,512]{1,0:T(8,128)(2,1)S(1)} collective-permute-done((bf16[256,512]{1,0:T(8,128)(2,1)S(1)}, bf16[256,512]{1,0:T(8,128)(2,1)S(1)}, u32[]{:S(2)}, u32[]{:S(2)}) %collective-permute-start.44) | collective-permute-done | bytes 262176 | tf_op jit(solution)/shard_map/ppermute | solution.py:261
  128.5 4.1 %collective-permute-start.41 = (bf16[256,512]{1,0:T(8,128)(2,1)S(1)}, bf16[256,512]{1,0:T(8,128)(2,1)S(1)}, u32[]{:S(2)}, u32[]{:S(2)}) collective-permute-start(bf16[256,512]{1,0:T(8,128)(2,1)S(1)} %collective-permute-done.36.refs_2_), channel_id=1, source_target_pairs={{0,8},{8,16},{16,24},{12,4},{20,12},{28,20},{1,9},{9,17},{17,25},{... | collective-permute-start | bytes 786440 | tf_op jit(solution)/shard_map/ppermute | solution.py:264
  133.2 4.0 %first.5.refs_8_ = f32[2,512,512]{2,1,0:T(8,128)S(1)} custom-call(s32[4]{0:T(128)S(1)} %copy-done.5, s32[16]{0:T(128)S(1)} %copy-done.6, bf16[256,512]{1,0:T(8,128)(2,1)S(1)} %get-tuple-element.61.refs_0_.refs_4_, bf16[256,512]{1,0:T(8,128)(2,1)S(1)} %collective-permute-done.32.refs_1_.refs_5_, bf16[256,512]{1,0:T(8,128)(2,1)S(1)} %collective-permute-done.42.refs_2_, ...), custom_call_target="tpu_custom_call" | custom-call | flops 2147483648 | bytes 7864400 | tf_op jit(solution)/shard_map/first/pallas_call | solution.py:35
  148.6 3.5 %collective-permute-start.49 = (f32[8,128]{1,0:T(8,128)S(1)}, f32[8,128]{1,0:T(8,128)S(1)}, u32[]{:S(2)}, u32[]{:S(2)}) collective-permute-start(f32[8,128]{1,0:T(8,128)S(1)} %add.75), channel_id=1, source_target_pairs={{0,16},{4,20},{8,24},{12,28},{16,0},{20,4},{24,8},{28,12},{1,17},{... | collective-permute-start | bytes 12296 | tf_op jit(solution)/shard_map/ppermute | solution.py:234
  155.9 4.0 %collective-permute-done.48.refs_1_ = bf16[256,512]{1,0:T(8,128)(2,1)S(1)} collective-permute-done((bf16[256,512]{1,0:T(8,128)(2,1)S(1)}, bf16[256,512]{1,0:T(8,128)(2,1)S(1)}, u32[]{:S(2)}, u32[]{:S(2)}) %collective-permute-start.48) | collective-permute-done | bytes 262176 | tf_op jit(solution)/shard_map/ppermute | solution.py:286
  170.3 3.0 %collective-permute-start.57 = (f32[8,128]{1,0:T(8,128)S(1)}, f32[8,128]{1,0:T(8,128)S(1)}, u32[]{:S(2)}, u32[]{:S(2)}) collective-permute-start(f32[8,128]{1,0:T(8,128)S(1)} %add.80), channel_id=1, source_target_pairs={{0,16},{4,20},{8,24},{12,28},{16,0},{20,4},{24,8},{28,12},{1,17},{... | collective-permute-start | bytes 12296 | tf_op jit(solution)/shard_map/ppermute | solution.py:234
  175.0 3.2 %last.1 = (bf16[2,512,512]{2,1,0:T(8,128)(2,1)}, f32[2,3]{1,0:T(2,128)}) custom-call(s32[4]{0:T(128)S(1)} %copy-done.5, s32[16]{0:T(128)S(1)} %copy-done.6, bf16[256,512]{1,0:T(8,128)(2,1)S(1)} %get-tuple-element.40.refs_0_.refs_2_, bf16[256,512]{1,0:T(8,128)(2,1)S(1)} %get-tuple-element.41.refs_1_, ...), custom_call_target="tpu_custom_call" | custom-call | bytes 4210768 | tf_op jit(solution)/shard_map/last/pallas_call | solution.py:35
  (148 shorter events, 88.6 us)
Async XLA Ops:
  3.9 9.4 %collective-permute-start.6 = (bf16[256,512]{1,0:T(8,128)(2,1)S(1)}, bf16[256,512]{1,0:T(8,128)(2,1)S(1)}, u32[]{:S(2)}, u32[]{:S(2)}) collective-permute-start(bf16[256,512]{1,0:T(8,128)(2,1)S(1)} %get-tuple-element.40.refs_0_.refs_2_), channel_id=1, source_target_pairs={{0,4},{4,0},{8,12},{12,8},{16,20},{20,16},{24,28},{28,24},{1,5},{5... | collective-permute-start | bytes 786440 | tf_op jit(solution)/shard_map/ppermute | solution.py:258
  17.1 8.7 %collective-permute-start = (bf16[256,512]{1,0:T(8,128)(2,1)S(1)}, bf16[256,512]{1,0:T(8,128)(2,1)S(1)}, u32[]{:S(2)}, u32[]{:S(2)}) collective-permute-start(bf16[256,512]{1,0:T(8,128)(2,1)S(1)} %get-tuple-element.42.refs_0_.refs_2_.refs_8_), channel_id=1, source_target_pairs={{0,4},{4,0},{8,12},{12,8},{16,20},{20,16},{24,28},{28,24},{1,5},{5... | collective-permute-start | bytes 786440 | tf_op jit(solution)/shard_map/ppermute | solution.py:259
  17.2 12.7 %collective-permute-start.7 = (bf16[256,512]{1,0:T(8,128)(2,1)S(1)}, bf16[256,512]{1,0:T(8,128)(2,1)S(1)}, u32[]{:S(2)}, u32[]{:S(2)}) collective-permute-start(bf16[256,512]{1,0:T(8,128)(2,1)S(1)} %collective-permute-done.6.refs_2_), channel_id=1, source_target_pairs={{0,1},{1,0},{2,3},{3,2},{4,5},{5,4},{6,7},{7,6},{8,9},{9,8},{10,11... | collective-permute-start | bytes 786440 | tf_op jit(solution)/shard_map/ppermute | solution.py:228
  25.8 11.8 %collective-permute-start.5 = (bf16[256,512]{1,0:T(8,128)(2,1)S(1)}, bf16[256,512]{1,0:T(8,128)(2,1)S(1)}, u32[]{:S(2)}, u32[]{:S(2)}) collective-permute-start(bf16[256,512]{1,0:T(8,128)(2,1)S(1)} %collective-permute-done.refs_2_), channel_id=1, source_target_pairs={{0,8},{8,16},{16,24},{12,4},{20,12},{28,20},{1,9},{9,17},{17,25},{... | collective-permute-start | bytes 786440 | tf_op jit(solution)/shard_map/ppermute | solution.py:264
  46.2 9.2 %collective-permute-start.12 = (bf16[256,512]{1,0:T(8,128)(2,1)S(1)}, bf16[256,512]{1,0:T(8,128)(2,1)S(1)}, u32[]{:S(2)}, u32[]{:S(2)}) collective-permute-start(bf16[256,512]{1,0:T(8,128)(2,1)S(1)} %add.82.refs_0_), channel_id=1, source_target_pairs={{0,2},{1,3},{2,0},{3,1},{4,6},{5,7},{6,4},{7,5},{8,10},{9,11},{10,... | collective-permute-start | bytes 786440 | tf_op jit(solution)/shard_map/ppermute | solution.py:286
  48.4 11.7 %collective-permute-start.16 = (bf16[256,512]{1,0:T(8,128)(2,1)S(1)}, bf16[256,512]{1,0:T(8,128)(2,1)S(1)}, u32[]{:S(2)}, u32[]{:S(2)}) collective-permute-start(bf16[256,512]{1,0:T(8,128)(2,1)S(1)} %add.83.refs_0_), channel_id=1, source_target_pairs={{0,2},{1,3},{2,0},{3,1},{4,6},{5,7},{6,4},{7,5},{8,10},{9,11},{10,... | collective-permute-start | bytes 786440 | tf_op jit(solution)/shard_map/ppermute | solution.py:286
  56.3 9.5 %collective-permute-start.24 = (bf16[256,512]{1,0:T(8,128)(2,1)S(1)}, bf16[256,512]{1,0:T(8,128)(2,1)S(1)}, u32[]{:S(2)}, u32[]{:S(2)}) collective-permute-start(bf16[256,512]{1,0:T(8,128)(2,1)S(1)} %get-tuple-element.50.refs_0_.refs_3_.refs_2_), channel_id=1, source_target_pairs={{0,4},{4,0},{8,12},{12,8},{16,20},{20,16},{24,28},{28,24},{1,5},{5... | collective-permute-start | bytes 786440 | tf_op jit(solution)/shard_map/ppermute | solution.py:258
  69.3 8.8 %collective-permute-start.18 = (bf16[256,512]{1,0:T(8,128)(2,1)S(1)}, bf16[256,512]{1,0:T(8,128)(2,1)S(1)}, u32[]{:S(2)}, u32[]{:S(2)}) collective-permute-start(bf16[256,512]{1,0:T(8,128)(2,1)S(1)} %get-tuple-element.53.refs_0_.refs_3_.refs_10_), channel_id=1, source_target_pairs={{0,4},{4,0},{8,12},{12,8},{16,20},{20,16},{24,28},{28,24},{1,5},{5... | collective-permute-start | bytes 786440 | tf_op jit(solution)/shard_map/ppermute | solution.py:259
  69.4 12.7 %collective-permute-start.14 = (bf16[256,512]{1,0:T(8,128)(2,1)S(1)}, bf16[256,512]{1,0:T(8,128)(2,1)S(1)}, u32[]{:S(2)}, u32[]{:S(2)}) collective-permute-start(bf16[256,512]{1,0:T(8,128)(2,1)S(1)} %get-tuple-element.50.refs_0_.refs_3_.refs_2_), channel_id=1, source_target_pairs={{0,1},{1,0},{2,3},{3,2},{4,5},{5,4},{6,7},{7,6},{8,9},{9,8},{10,11... | collective-permute-start | bytes 786440 | tf_op jit(solution)/shard_map/ppermute | solution.py:228
  69.5 13.2 %collective-permute-start.25 = (bf16[256,512]{1,0:T(8,128)(2,1)S(1)}, bf16[256,512]{1,0:T(8,128)(2,1)S(1)}, u32[]{:S(2)}, u32[]{:S(2)}) collective-permute-start(bf16[256,512]{1,0:T(8,128)(2,1)S(1)} %collective-permute-done.24.refs_2_), channel_id=1, source_target_pairs={{0,1},{1,0},{2,3},{3,2},{4,5},{5,4},{6,7},{7,6},{8,9},{9,8},{10,11... | collective-permute-start | bytes 786440 | tf_op jit(solution)/shard_map/ppermute | solution.py:228
  78.1 9.0 %collective-permute-start.23 = (bf16[256,512]{1,0:T(8,128)(2,1)S(1)}, bf16[256,512]{1,0:T(8,128)(2,1)S(1)}, u32[]{:S(2)}, u32[]{:S(2)}) collective-permute-start(bf16[256,512]{1,0:T(8,128)(2,1)S(1)} %collective-permute-done.18.refs_2_), channel_id=1, source_target_pairs={{0,8},{8,16},{16,24},{12,4},{20,12},{28,20},{1,9},{9,17},{17,25},{... | collective-permute-start | bytes 786440 | tf_op jit(solution)/shard_map/ppermute | solution.py:264
  95.5 9.2 %collective-permute-start.30 = (bf16[256,512]{1,0:T(8,128)(2,1)S(1)}, bf16[256,512]{1,0:T(8,128)(2,1)S(1)}, u32[]{:S(2)}, u32[]{:S(2)}) collective-permute-start(bf16[256,512]{1,0:T(8,128)(2,1)S(1)} %add.84.refs_0_), channel_id=1, source_target_pairs={{0,2},{1,3},{2,0},{3,1},{4,6},{5,7},{6,4},{7,5},{8,10},{9,11},{10,... | collective-permute-start | bytes 786440 | tf_op jit(solution)/shard_map/ppermute | solution.py:286
  97.7 11.7 %collective-permute-start.34 = (bf16[256,512]{1,0:T(8,128)(2,1)S(1)}, bf16[256,512]{1,0:T(8,128)(2,1)S(1)}, u32[]{:S(2)}, u32[]{:S(2)}) collective-permute-start(bf16[256,512]{1,0:T(8,128)(2,1)S(1)} %add.85.refs_0_), channel_id=1, source_target_pairs={{0,2},{1,3},{2,0},{3,1},{4,6},{5,7},{6,4},{7,5},{8,10},{9,11},{10,... | collective-permute-start | bytes 786440 | tf_op jit(solution)/shard_map/ppermute | solution.py:286
  105.7 9.5 %collective-permute-start.42 = (bf16[256,512]{1,0:T(8,128)(2,1)S(1)}, bf16[256,512]{1,0:T(8,128)(2,1)S(1)}, u32[]{:S(2)}, u32[]{:S(2)}) collective-permute-start(bf16[256,512]{1,0:T(8,128)(2,1)S(1)} %get-tuple-element.61.refs_0_.refs_4_), channel_id=1, source_target_pairs={{0,4},{4,0},{8,12},{12,8},{16,20},{20,16},{24,28},{28,24},{1,5},{5... | collective-permute-start | bytes 786440 | tf_op jit(solution)/shard_map/ppermute | solution.py:258
  115.3 9.1 %collective-permute-start.44 = (bf16[256,512]{1,0:T(8,128)(2,1)S(1)}, bf16[256,512]{1,0:T(8,128)(2,1)S(1)}, u32[]{:S(2)}, u32[]{:S(2)}) collective-permute-start(bf16[256,512]{1,0:T(8,128)(2,1)S(1)} %collective-permute-done.42.refs_2_), channel_id=1, source_target_pairs={{0,8},{8,16},{16,24},{12,4},{20,12},{28,20},{1,9},{9,17},{17,25},{... | collective-permute-start | bytes 786440 | tf_op jit(solution)/shard_map/ppermute | solution.py:261
  119.7 8.8 %collective-permute-start.36 = (bf16[256,512]{1,0:T(8,128)(2,1)S(1)}, bf16[256,512]{1,0:T(8,128)(2,1)S(1)}, u32[]{:S(2)}, u32[]{:S(2)}) collective-permute-start(bf16[256,512]{1,0:T(8,128)(2,1)S(1)} %get-tuple-element.64.refs_0_.refs_4_.refs_12_), channel_id=1, source_target_pairs={{0,4},{4,0},{8,12},{12,8},{16,20},{20,16},{24,28},{28,24},{1,5},{5... | collective-permute-start | bytes 786440 | tf_op jit(solution)/shard_map/ppermute | solution.py:259
  119.8 12.9 %collective-permute-start.32 = (bf16[256,512]{1,0:T(8,128)(2,1)S(1)}, bf16[256,512]{1,0:T(8,128)(2,1)S(1)}, u32[]{:S(2)}, u32[]{:S(2)}) collective-permute-start(bf16[256,512]{1,0:T(8,128)(2,1)S(1)} %get-tuple-element.61.refs_0_.refs_4_), channel_id=1, source_target_pairs={{0,1},{1,0},{2,3},{3,2},{4,5},{5,4},{6,7},{7,6},{8,9},{9,8},{10,11... | collective-permute-start | bytes 786440 | tf_op jit(solution)/shard_map/ppermute | solution.py:228
  119.8 13.3 %collective-permute-start.43 = (bf16[256,512]{1,0:T(8,128)(2,1)S(1)}, bf16[256,512]{1,0:T(8,128)(2,1)S(1)}, u32[]{:S(2)}, u32[]{:S(2)}) collective-permute-start(bf16[256,512]{1,0:T(8,128)(2,1)S(1)} %collective-permute-done.42.refs_2_), channel_id=1, source_target_pairs={{0,1},{1,0},{2,3},{3,2},{4,5},{5,4},{6,7},{7,6},{8,9},{9,8},{10,11... | collective-permute-start | bytes 786440 | tf_op jit(solution)/shard_map/ppermute | solution.py:228
  124.4 8.8 %collective-permute-start.45 = (bf16[256,512]{1,0:T(8,128)(2,1)S(1)}, bf16[256,512]{1,0:T(8,128)(2,1)S(1)}, u32[]{:S(2)}, u32[]{:S(2)}) collective-permute-start(bf16[256,512]{1,0:T(8,128)(2,1)S(1)} %collective-permute-done.44.refs_4_), channel_id=1, source_target_pairs={{0,1},{1,0},{2,3},{3,2},{4,5},{5,4},{6,7},{7,6},{8,9},{9,8},{10,11... | collective-permute-start | bytes 786440 | tf_op jit(solution)/shard_map/ppermute | solution.py:228
  128.5 9.0 %collective-permute-start.41 = (bf16[256,512]{1,0:T(8,128)(2,1)S(1)}, bf16[256,512]{1,0:T(8,128)(2,1)S(1)}, u32[]{:S(2)}, u32[]{:S(2)}) collective-permute-start(bf16[256,512]{1,0:T(8,128)(2,1)S(1)} %collective-permute-done.36.refs_2_), channel_id=1, source_target_pairs={{0,8},{8,16},{16,24},{12,4},{20,12},{28,20},{1,9},{9,17},{17,25},{... | collective-permute-start | bytes 786440 | tf_op jit(solution)/shard_map/ppermute | solution.py:264
  145.5 9.2 %collective-permute-start.52 = (bf16[256,512]{1,0:T(8,128)(2,1)S(1)}, bf16[256,512]{1,0:T(8,128)(2,1)S(1)}, u32[]{:S(2)}, u32[]{:S(2)}) collective-permute-start(bf16[256,512]{1,0:T(8,128)(2,1)S(1)} %add.87.refs_0_), channel_id=1, source_target_pairs={{0,2},{1,3},{2,0},{3,1},{4,6},{5,7},{6,4},{7,5},{8,10},{9,11},{10,... | collective-permute-start | bytes 786440 | tf_op jit(solution)/shard_map/ppermute | solution.py:286
  147.7 12.2 %collective-permute-start.48 = (bf16[256,512]{1,0:T(8,128)(2,1)S(1)}, bf16[256,512]{1,0:T(8,128)(2,1)S(1)}, u32[]{:S(2)}, u32[]{:S(2)}) collective-permute-start(bf16[256,512]{1,0:T(8,128)(2,1)S(1)} %add.86.refs_0_), channel_id=1, source_target_pairs={{0,2},{1,3},{2,0},{3,1},{4,6},{5,7},{6,4},{7,5},{8,10},{9,11},{10,... | collective-permute-start | bytes 786440 | tf_op jit(solution)/shard_map/ppermute | solution.py:286
  155.8 19.1 %collective-permute-start.53 = (bf16[256,512]{1,0:T(8,128)(2,1)S(1)}, bf16[256,512]{1,0:T(8,128)(2,1)S(1)}, u32[]{:S(2)}, u32[]{:S(2)}) collective-permute-start(bf16[256,512]{1,0:T(8,128)(2,1)S(1)} %get-tuple-element.75.refs_14_), channel_id=1, source_target_pairs={{0,1},{1,0},{2,3},{3,2},{4,5},{5,4},{6,7},{7,6},{8,9},{9,8},{10,11... | collective-permute-start | bytes 786440 | tf_op jit(solution)/shard_map/ppermute | solution.py:228
  161.0 13.9 %collective-permute-start.50 = (bf16[256,512]{1,0:T(8,128)(2,1)S(1)}, bf16[256,512]{1,0:T(8,128)(2,1)S(1)}, u32[]{:S(2)}, u32[]{:S(2)}) collective-permute-start(bf16[256,512]{1,0:T(8,128)(2,1)S(1)} %get-tuple-element.72.refs_6_), channel_id=1, source_target_pairs={{0,1},{1,0},{2,3},{3,2},{4,5},{5,4},{6,7},{7,6},{8,9},{9,8},{10,11... | collective-permute-start | bytes 786440 | tf_op jit(solution)/shard_map/ppermute | solution.py:228
  (41 other events, 161.4 us)
